TPU v7x, 512 devices: a whole 4x8x8 slice. The times are simulated.
512 devices in a mesh: row: 32 (over x, z), col: 16 (over y, core).
Axes of the slice: x: 4, y: 8, z: 8, core: 2. Of those that a mesh axis runs over, the one named last changes fastest.
Arguments:
- eigvectors: bfloat16 [98304, 2048], P('row', 'col'), may hold values from -0.4375 to 0.4375
- panel_vectors: bfloat16 [2, 256, 98304], P(None, 'col', 'row'), may hold values from -0.21875 to 0.21875
- panel_factors: float32 [2, 256, 256], replicated, may hold values from -0.375 to 0.375
- eigenvalues: float32 [2048], replicated, may hold values from 4 to 400
- damping: float32 [2048], replicated, may hold values from 0.02 to 0.1
- frequencies: float32 [8], replicated, may hold values from 4 to 16
- loads: bfloat16 [64, 98304], P(None, ('row', 'col')), may hold values from -6 to 6
Outputs:
- resp_real: bfloat16 [8, 64, 98304], P(None, None, ('row', 'col'))
- resp_imag: bfloat16 [8, 64, 98304], P(None, None, ('row', 'col'))
All inputs are finite; a program needn't handle non-finite values.
Results may differ from a plain program's by a relative error of at most 0.015.
Values may be sent and summed in bfloat16 or wider, within the bound.
No kernel may reach another device: no remote copies, remote signals or barrier semaphores. Data moves between devices by JAX's collectives and lax.ppermute only.
A program may use at most 64 MiB of HBM per device.

v0:
```python
import jax
import jax.numpy as jnp
from jax import lax
from jax.sharding import PartitionSpec as P


def transfer(eigenvalues, damping, frequencies):
    detune = eigenvalues[None, :] - frequencies[:, None] * frequencies[:, None]
    width = 2.0 * damping[None, :] * frequencies[:, None] * jnp.sqrt(eigenvalues)[None, :]
    denom = detune * detune + width * width
    return (detune / denom, -width / denom)


def apply_back(vectors, factor_rows):
    return lax.dot_general(
        vectors, factor_rows, (((0,), (0,)), ((), ())), preferred_element_type=jnp.float32
    )


def body(eigvectors, panel_vectors, panel_factors, eigenvalues, damping, frequencies, loads):
    highest = lax.Precision.HIGHEST
    upper = jnp.triu(panel_factors)
    vectors = lax.all_gather(panel_vectors, "col", axis=1, tiled=True)
    first = vectors[0]
    second = vectors[1]

    def panel_total(partial_value):
        return lax.psum(partial_value, "row")

    w_first = panel_total(jnp.dot(first, eigvectors, preferred_element_type=jnp.float32))
    y_first = jnp.dot(upper[0].T, w_first, precision=highest).astype(jnp.bfloat16)
    z_first = eigvectors.astype(jnp.float32) - apply_back(first, y_first)
    w_second = panel_total(jnp.dot(second.astype(jnp.float32), z_first, precision=highest))
    y_second = jnp.dot(upper[1].T, w_second, precision=highest).astype(jnp.bfloat16)
    rotated = (z_first - apply_back(second, y_second)).astype(jnp.bfloat16)
    all_modes = lax.all_to_all(rotated, "col", split_axis=0, concat_axis=1, tiled=True)
    partial_modal = jnp.dot(loads, all_modes, preferred_element_type=jnp.float32)
    modal = lax.psum(partial_modal, ("row", "col"))
    h_real, h_imag = transfer(eigenvalues, damping, frequencies)
    real_parts = []
    imag_parts = []
    for index in range(frequencies.shape[0]):
        scaled_re = (modal * h_real[index][None, :]).astype(jnp.bfloat16)
        scaled_im = (modal * h_imag[index][None, :]).astype(jnp.bfloat16)
        stacked = jnp.concatenate([scaled_re, scaled_im], axis=0)
        product = lax.dot_general(
            stacked, all_modes, (((1,), (1,)), ((), ())), preferred_element_type=jnp.float32
        )
        half = scaled_re.shape[0]
        real_parts.append(product[:half].astype(jnp.bfloat16))
        imag_parts.append(product[half:].astype(jnp.bfloat16))
    return (jnp.stack(real_parts), jnp.stack(imag_parts))


def solution(mesh):
    return jax.shard_map(
        body,
        mesh=mesh,
        in_specs=(
            P("row", "col"),
            P(None, "col", "row"),
            P(),
            P(),
            P(),
            P(),
            P(None, ("row", "col")),
        ),
        out_specs=(P(None, None, ("row", "col")), P(None, None, ("row", "col"))),
        check_vma=False,
    )
```

profile of v0, /device:TPU:1, one launch (start us, length us, event | category | flops | bytes accessed | tf_op | source)
XLA Modules:
  0.0 683.9 jit_solution(8062973324955256329)
XLA Ops:
  7.2 0.0 copy-start
  7.2 0.0 copy-start.2
  7.2 0.0 all-gather.2.cloned.1.call-start
  7.2 0.7 all-gather.2.cloned.1.call-update
  7.9 0.0 all-reduce.4.cloned.1.call-start
  8.0 1.4 copy.12
  9.4 0.0 copy-start.3
  9.4 0.1 iota_compare_fusion
  9.5 50.1 %all-gather.2.cloned.1.call-done = bf16[2,256,3072]{2,1,0:T(8,128)(2,1)} async-done(((bf16[2,16,3072]{2,1,0:T(8,128)(2,1)}), bf16[2,256,3072]{2,1,0:T(8,128)(2,1)}) %all-gather.2.cloned.1.call-update) | async-done | bytes 3145744 | tf_op jit(solution)/shard_map/all_gather | solution.py:23
  59.6 0.0 copy-done.2
  59.6 2.6 fusion.3
  62.2 0.0 all-reduce.4.cloned.1.call-update
  62.3 0.0 all-reduce.6.cloned.1.call-start
  62.3 0.0 copy-done.3
  62.3 0.1 broadcast_select_fusion
  62.4 147.8 %all-reduce.4.cloned.1.call-done = f32[256,128]{1,0:T(8,128)} async-done(((f32[256,128]{1,0:T(8,128)}), f32[256,128]{1,0:T(8,128)}) %all-reduce.4.cloned.1.call-update) | async-done | bytes 131088 | tf_op jit(solution)/shard_map/psum | solution.py:28
  210.2 1.5 convolution_convert_fusion.1
  211.7 0.0 copy-start.1
  211.7 2.0 fusion.1
  213.7 0.4 copy-done.1
  214.0 2.4 fusion.5
  216.4 0.0 all-reduce.6.cloned.1.call-update
  216.4 150.2 %all-reduce.6.cloned.1.call-done = f32[256,128]{0,1:T(8,128)} async-done(((f32[256,128]{0,1:T(8,128)}), f32[256,128]{0,1:T(8,128)}) %all-reduce.6.cloned.1.call-update) | async-done | bytes 131088 | tf_op jit(solution)/shard_map/psum | solution.py:28
  366.6 1.5 convolution_convert_fusion
  368.1 1.8 fusion.2
  370.0 0.0 copy-start.4
  370.0 0.0 copy-start.6
  370.0 0.0 copy-start.5
  370.0 1.2 copy.13
  371.2 11.5 %all-to-all-start = ((bf16[16,192,128]{2,1,0:T(8,128)(2,1)}), bf16[16,192,128]{2,1,0:T(8,128)(2,1)S(1)}, u32[]{:S(2)}, u32[]{:S(2)}) async-start(bf16[16,192,128]{2,1,0:T(8,128)(2,1)} %bitcast.7), calls=%async_computation | async-start | bytes 1572864 | tf_op jit(solution)/shard_map/all_to_all | solution.py:36
  382.7 0.0 all-reduce.8.cloned.1.call-start
  382.7 0.0 copy-done.4
  382.7 0.0 copy-done.6
  382.8 0.0 copy-done.5
  382.8 0.1 subtract_divide_fusion
  382.9 22.4 %all-to-all-done = bf16[16,192,128]{2,1,0:T(8,128)(2,1)S(1)} async-done(((bf16[16,192,128]{2,1,0:T(8,128)(2,1)}), bf16[16,192,128]{2,1,0:T(8,128)(2,1)S(1)}, u32[]{:S(2)}, u32[]{:S(2)}) %all-to-all-start) | async-done | bytes 786464 | tf_op jit(solution)/shard_map/all_to_all | solution.py:36
  405.3 0.0 copy-done
  405.3 1.1 convolution_bitcast_fusion.2
  406.4 0.0 all-reduce.8.cloned.1.call-update
  406.4 0.1 fusion.73
  406.5 263.2 %all-reduce.8.cloned.1.call-done = f32[64,2048]{1,0:T(8,128)} async-done(((f32[64,2048]{1,0:T(8,128)}), f32[64,2048]{1,0:T(8,128)}) %all-reduce.8.cloned.1.call-update) | async-done | bytes 524304 | tf_op jit(solution)/shard_map/psum | solution.py:38
  669.7 2.0 multiply_convert_fusion.1
  671.7 0.4 convolution_convert_fusion.9
  672.1 0.1 fusion.47
  672.2 0.4 convolution_convert_fusion.8
  672.5 0.1 fusion.46
  672.6 0.4 convolution_convert_fusion.7
  673.0 0.1 fusion.45
  673.1 0.4 convolution_convert_fusion.6
  673.5 0.1 fusion.44
  673.6 0.4 convolution_convert_fusion.5
  674.0 0.1 fusion.43
  674.1 0.4 convolution_convert_fusion.4
  674.5 0.1 fusion.42
  674.6 0.4 convolution_convert_fusion.3
  674.9 0.1 fusion.41
  675.0 0.4 convolution_convert_fusion.2
  675.4 0.1 fusion.40
  675.5 0.9 copy.15
  676.4 0.9 copy.16
  (4 shorter events, 0.0 us)
Async XLA Ops:
  7.2 398.2 %copy-start = (bf16[64,192]{1,0:T(8,128)(2,1)S(1)}, bf16[64,192]{1,0:T(8,128)(2,1)}, u32[]{:S(2)}) copy-start(bf16[64,192]{1,0:T(8,128)(2,1)} %param.13) | copy-start | bytes 73732
  7.2 52.4 %copy-start.2 = (bf16[3072,128]{1,0:T(8,128)(2,1)S(1)}, bf16[3072,128]{1,0:T(8,128)(2,1)}, u32[]{:S(2)}) copy-start(bf16[3072,128]{1,0:T(8,128)(2,1)} %param.7) | copy-start | bytes 2359300
  7.2 52.4 %all-gather.2.cloned.1.call-start = ((), (), s32[]{:S(2)}) async-start(), calls=%async_computation.1 | async-start | bytes 3342336 | tf_op jit(solution)/shard_map/all_gather | solution.py:23
  7.9 202.3 %all-reduce.4.cloned.1.call-start = ((), (), s32[]{:S(2)}) async-start(), calls=%async_computation.2 | async-start | bytes 262144 | tf_op jit(solution)/shard_map/psum | solution.py:28
  9.4 52.9 %copy-start.3 = (f32[2,256,256]{2,1,0:T(8,128)S(1)}, f32[2,256,256]{2,1,0:T(8,128)}, u32[]{:S(2)}) copy-start(f32[2,256,256]{2,1,0:T(8,128)} %param.9) | copy-start | bytes 1572868
  62.3 304.4 %all-reduce.6.cloned.1.call-start = ((), (), s32[]{:S(2)}) async-start(), calls=%async_computation.3 | async-start | bytes 262144 | tf_op jit(solution)/shard_map/psum | solution.py:28
  211.7 2.4 copy-start.1
  370.0 12.8 %copy-start.4 = (f32[2048]{0:T(1024)S(1)}, f32[2048]{0:T(1024)}, u32[]{:S(2)}) copy-start(f32[2048]{0:T(1024)} %param.10) | copy-start | bytes 24580
  370.0 12.8 %copy-start.6 = (f32[8]{0:T(128)S(1)}, f32[8]{0:T(128)}, u32[]{:S(2)}) copy-start(f32[8]{0:T(128)} %param.12) | copy-start | bytes 100
  370.0 12.8 %copy-start.5 = (f32[2048]{0:T(1024)S(1)}, f32[2048]{0:T(1024)}, u32[]{:S(2)}) copy-start(f32[2048]{0:T(1024)} %param.11) | copy-start | bytes 24580
  371.2 34.2 %all-to-all-start = ((bf16[16,192,128]{2,1,0:T(8,128)(2,1)}), bf16[16,192,128]{2,1,0:T(8,128)(2,1)S(1)}, u32[]{:S(2)}, u32[]{:S(2)}) async-start(bf16[16,192,128]{2,1,0:T(8,128)(2,1)} %bitcast.7), calls=%async_computation | async-start | bytes 1572864 | tf_op jit(solution)/shard_map/all_to_all | solution.py:36
  382.7 287.0 %all-reduce.8.cloned.1.call-start = ((), (), s32[]{:S(2)}) async-start(), calls=%async_computation.4 | async-start | bytes 1048576 | tf_op jit(solution)/shard_map/psum | solution.py:38
Sparse Core Ops, SparseCore 0:
  10.2 49.4 all-gather.1
  63.6 146.4 all-reduce.3
  216.6 150.0 all-reduce.5
  406.5 263.0 all-reduce.7
where the time goes:
time: 684 us
  waiting for transfers between devices  634 us (93%)
  matrix products  15.8 us (2%)
  between operations  14 us (2%)
  starting transfers between devices  11.7 us (2%)
    psum x2, waiting for transfers between devices, panel_total(): return lax.psum(partial_value, 'row')  298 us
    psum x1, waiting for transfers between devices, body(): modal = lax.psum(partial_modal, ('row', 'col'))  263 us
    all_gather x1, waiting for transfers between devices, body(): vectors = lax.all_gather(panel_vectors, 'col', axis=1, tiled=True)  50.1 us
    all_to_all x1, waiting for transfers between devices, body(): lax.all_to_all(rotated, 'col', split_axis=0, concat_axis=1, tiled=True)  22.4 us
  transfers between devices with their start and end apart: 5, of which 5 were waited for; matrix products, arithmetic and copies ran while one was open for 0% of the time, Pallas kernels for 0%

commit v1 on v0

v1 whole, which is shorter than its diff:
```python
import jax
import jax.numpy as jnp
from jax import lax
from jax.sharding import PartitionSpec as P

HIGHEST = lax.Precision.HIGHEST


def transfer(eigenvalues, damping, frequencies):
    detune = eigenvalues[None, :] - frequencies[:, None] * frequencies[:, None]
    width = 2.0 * damping[None, :] * frequencies[:, None] * jnp.sqrt(eigenvalues)[None, :]
    denom = detune * detune + width * width
    return (detune / denom, -width / denom)


def exchange(chunks, axis):
    return lax.all_to_all(chunks, axis, split_axis=0, concat_axis=0, tiled=True)


def spread(value, axis, count):
    return exchange(jnp.broadcast_to(value[None], (count,) + value.shape), axis)


def dot32(left, right, dims):
    return lax.dot_general(left, right, (dims, ((), ())), preferred_element_type=jnp.float32)


def exact(left, right, dims):
    return lax.dot_general(left, right, (dims, ((), ())), precision=HIGHEST)


def body(eigvectors, panel_vectors, panel_factors, eigenvalues, damping, frequencies, loads):
    rows = lax.axis_size("row")
    cols = lax.axis_size("col")
    bf16 = jnp.bfloat16
    _, mine, dofs = panel_vectors.shape
    modes = eigvectors.shape[1]
    cases, block = loads.shape
    size = panel_factors.shape[-1]
    upper = jnp.triu(panel_factors)

    half = cases // 2
    folded = jnp.concatenate([loads[:half], loads[half:]], axis=1).reshape(2, mine, 2 * block)
    packed = jnp.concatenate([panel_vectors, folded], axis=2)
    gathered = lax.all_gather(packed, "col", axis=1, tiled=True)
    vectors = gathered[:, :, :dofs]

    cut = panel_vectors.reshape(2 * mine, cols, block).transpose(1, 0, 2)
    cut = exchange(cut, "col").reshape(cols, 2, mine, block).transpose(1, 0, 2, 3)
    cut = cut.reshape(2, size, block)
    last = ((1,), (1,))
    second_loads = jnp.concatenate([cut[1], loads], axis=0)
    gram = jnp.concatenate([dot32(second_loads, cut[0], last), dot32(loads, cut[1], last)], axis=0)
    wide = gram.shape[1] // 2
    gram = jnp.concatenate([gram[:, :wide], gram[:, wide:]], axis=0)
    piece = gram.shape[0] // rows
    gram = jnp.sum(exchange(gram.reshape(rows, piece, wide), "row"), axis=0)
    gram = jnp.sum(spread(gram, "col", cols), axis=0)

    tail = gathered[:, :, dofs:].reshape(2, cols, mine, 2, block)
    tail = tail.transpose(3, 0, 2, 1, 4).reshape(cases, dofs)
    panels = dot32(eigvectors, vectors, ((0,), (2,))).reshape(modes, 2 * size)
    direct = dot32(eigvectors, tail, ((0,), (1,)))
    part = jnp.concatenate([panels, direct], axis=1)
    width = part.shape[1]
    share = modes // rows
    part = part.reshape(rows, share * width)
    sent = jnp.concatenate([part, jnp.broadcast_to(gram.reshape(1, -1), (rows, piece * wide))], axis=1)
    got = exchange(sent.reshape(rows, -1, 128), "row").reshape(rows, -1)
    total = jnp.sum(got[:, : share * width].reshape(rows, share, width), axis=0)
    gram = got[:, share * width :].reshape(2, rows * piece // 2, wide)
    gram = jnp.concatenate([gram[0], gram[1]], axis=1)

    inner = ((1,), (0,))
    y_first = exact(total[:, :size], upper[0], inner).astype(bf16)
    first32 = y_first.astype(jnp.float32)
    other = total[:, size:] - exact(first32, gram[: size + cases], last)
    y_second = exact(other[:, :size], upper[1], inner).astype(bf16)
    modal = other[:, size:] - exact(y_second.astype(jnp.float32), gram[size + cases :], last)
    answer = jnp.concatenate([y_first, y_second, modal.astype(bf16)], axis=1)
    answer = spread(answer.reshape(-1, 128), "row", rows).reshape(modes, width)

    weights = answer[:, : 2 * size].reshape(modes, 2, size)
    applied = dot32(vectors, weights, ((0, 1), (1, 2)))
    rotated = (eigvectors.astype(jnp.float32) - applied).astype(bf16)
    own_modal = answer[:, 2 * size :].T
    sent = jnp.concatenate(
        [rotated.reshape(cols, block, modes), jnp.broadcast_to(own_modal[None], (cols, cases, modes))], axis=1
    )
    got = exchange(sent, "col")
    all_modes = got[:, :block]
    all_modal = got[:, block:].astype(jnp.float32)

    h_real, h_imag = transfer(eigenvalues, damping, frequencies)
    count = frequencies.shape[0]
    scale = jnp.stack([h_real, h_imag]).reshape(2, count, cols, 1, modes)
    scaled = (all_modal[None, None] * scale).astype(bf16)
    product = lax.dot_general(
        scaled, all_modes, (((2, 4), (0, 2)), ((), ())), preferred_element_type=jnp.float32
    ).astype(bf16)
    return (product[0], product[1])


def solution(mesh):
    return jax.shard_map(
        body,
        mesh=mesh,
        in_specs=(
            P("row", "col"),
            P(None, "col", "row"),
            P(),
            P(),
            P(),
            P(),
            P(None, ("row", "col")),
        ),
        out_specs=(P(None, None, ("row", "col")), P(None, None, ("row", "col"))),
        check_vma=False,
    )
```

time: 684 us -> 174 us (0.25)
  waiting for transfers between devices: 634 us -> 49.3 us
  blocking collectives: 0 us -> 76.9 us
    psum x3 -> x0, waiting for transfers between devices: 561 us -> none  [the longest x2 298 us: panel_total(): return lax.psum(partial_value, 'row')]
    all_to_all x0 -> x4, blocking collectives: none -> 76.9 us  [exchange(): return lax.all_to_all(chunks, axis, split_axis=0, concat_axis=0, tiled=True)]
    all_gather x1, waiting for transfers between devices: 50.1 us -> 0.02 us  [body(): gathered = lax.all_gather(packed, 'col', axis=1, tiled=True)]
    all_to_all x1 -> x2, waiting for transfers between devices: 22.4 us -> 49.2 us  [exchange(): return lax.all_to_all(chunks, axis, split_axis=0, concat_axis=0, tiled=True)]
    dot_general x15 -> x10, matrix products: 15.8 us -> 10.1 us  [the longest x5 8.02 us: dot32(): lax.dot_general(left, right, (dims, ((), ())), preferred_element_type=jnp...]
  transfers between devices with their start and end apart: 5 -> 3, of which waited for: 5 -> 2; matrix products, arithmetic and copies ran while one was open for 0% -> 2% of each run, Pallas kernels for 0% -> 0%
where the time goes in v1:
time: 174 us; the launch traced here: 173 us
  blocking collectives  76.9 us (44%)
  waiting for transfers between devices  49.3 us (28%)
  between operations  14.4 us (8%)
  starting transfers between devices  11.6 us (7%)
  matrix products  10.1 us (6%)
  local copies, waits for them, and re-layouts  7.48 us (4%)
  other arithmetic  3.32 us (2%)
    all_to_all x4, blocking collectives, exchange(): return lax.all_to_all(chunks, axis, split_axis=0, concat_axis=0, tiled=True)  76.9 us
    all_to_all x2, waiting for transfers between devices, exchange(): return lax.all_to_all(chunks, axis, split_axis=0, concat_axis=0, tiled=True)  49.2 us
    all_to_all x2, starting transfers between devices, exchange(): return lax.all_to_all(chunks, axis, split_axis=0, concat_axis=0, tiled=True)  11.6 us
    dot_general x5, matrix products, dot32(): lax.dot_general(left, right, (dims, ((), ())), preferred_element_type=jnp...  8.02 us
  transfers between devices with their start and end apart: 3, of which 2 were waited for; matrix products, arithmetic and copies ran while one was open for 2% of the time, Pallas kernels for 0%

profile of v1, /device:TPU:1, one launch (start us, length us, event | category | flops | bytes accessed | tf_op | source)
XLA Modules:
  0.0 173.2 jit_solution(6828958106231136998)
XLA Ops:
  7.2 0.0 all-gather.2.cloned.1.call-start
  7.2 0.7 fusion.26
  8.0 0.1 pad_maximum_fusion.5
  8.0 1.6 pad_maximum_fusion.4
  9.7 0.0 all-gather.2.cloned.1.call-update
  9.7 1.3 reshape.194
  10.9 0.1 copy.43
  11.0 21.2 %all_to_all.30 = bf16[16,32,192]{2,1,0:T(8,128)(2,1)S(1)} all-to-all(bf16[16,32,192]{2,1,0:T(8,128)(2,1)S(1)} %copy.43), channel_id=1, replica_groups=mesh['row'=32,'col'=16] {'col'}, dimensions={0} | all-to-all | bytes 393216 | tf_op jit(solution)/shard_map/all_to_all | solution.py:17
  32.2 0.9 fusion.27
  33.1 1.0 fusion.15
  34.2 0.0 copy-start
  34.2 25.2 %all_to_all.31 = f32[32,24,128]{2,1,0:T(8,128)S(1)} all-to-all(f32[32,24,128]{2,1,0:T(8,128)S(1)} %bitcast.75), channel_id=1, replica_groups=mesh['row'=32,'col'=16] {'row'}, dimensions={0} | all-to-all | bytes 786432 | tf_op jit(solution)/shard_map/all_to_all | solution.py:17
  59.5 14.9 %all_to_all.32 = f32[16,24,128]{2,1,0:T(8,128)S(1)} all-to-all(f32[16,24,128]{2,1,0:T(8,128)S(1)} %broadcast_in_dim.20), channel_id=1, replica_groups=mesh['row'=32,'col'=16] {'col'}, dimensions={0} | all-to-all | bytes 393216 | tf_op jit(solution)/shard_map/all_to_all | solution.py:17
  74.4 0.0 all-gather.2.cloned.1.call-done
  74.5 1.0 slice.109
  75.5 0.3 reshape.191
  75.8 0.3 copy.56
  76.1 0.5 reshape.192
  76.6 0.0 copy-done
  76.6 0.3 convolution_bitcast_fusion.1
  76.9 0.1 copy.42
  77.0 2.9 %fusion.6 = f32[2,256,128]{2,1,0:T(8,128)S(1)} fusion(bf16[2,256,3456]{2,1,0:T(8,128)(2,1)} %all-gather.2.cloned.1.call-done, bf16[3072,128]{1,0:T(8,128)(2,1)S(1)} %copy-done), kind=kOutput, calls=%fused_computation.8 | convolution fusion | flops 402653184 | bytes 4194304 | tf_op jit(solution)/shard_map/dot_general | solution.py:25
  79.9 0.0 copy-start.1
  79.9 0.1 copy.41
  80.1 0.1 reshape.193
  80.2 0.1 pad_maximum_fusion.1
  80.3 1.0 reshape.197
  81.3 5.3 %all-to-all-start.3 = ((f32[32,42,128]{2,1,0:T(8,128)}), f32[32,42,128]{2,1,0:T(8,128)S(1)}, u32[]{:S(2)}, u32[]{:S(2)}) async-start(f32[32,42,128]{2,1,0:T(8,128)} %reshape.197), calls=%async_computation.3 | async-start | bytes 1572864 | tf_op jit(solution)/shard_map/all_to_all | solution.py:17
  86.6 0.1 iota_compare_fusion
  86.7 0.0 copy-done.1
  86.7 0.1 broadcast_select_fusion
  86.8 21.4 %all-to-all-done.3 = f32[32,42,128]{2,1,0:T(8,128)S(1)} async-done(((f32[32,42,128]{2,1,0:T(8,128)}), f32[32,42,128]{2,1,0:T(8,128)S(1)}, u32[]{:S(2)}, u32[]{:S(2)}) %all-to-all-start.3) | async-done | bytes 688160 | tf_op jit(solution)/shard_map/all_to_all | solution.py:17
  108.2 0.2 copy.55
  108.6 0.1 reduce_sum.32
  108.7 0.2 convolution_convert_fusion.1
  108.9 0.3 convolution_subtract_fusion
  109.2 0.2 convolution_convert_fusion
  109.4 0.2 fusion.10
  109.6 0.1 broadcast_in_dim.46
  109.8 15.7 %all_to_all.33 = bf16[32,18,128]{2,1,0:T(8,128)(2,1)S(1)} all-to-all(bf16[32,18,128]{2,1,0:T(8,128)(2,1)S(1)} %broadcast_in_dim.47), channel_id=1, replica_groups=mesh['row'=32,'col'=16] {'row'}, dimensions={0} | all-to-all | bytes 294912 | tf_op jit(solution)/shard_map/all_to_all | solution.py:17
  125.5 0.2 reshape.199
  125.7 0.1 copy.44
  125.8 0.1 copy.47
  125.9 2.9 %fusion.4 = bf16[3072,128]{1,0:T(8,128)(2,1)S(1)} fusion(bf16[128,2,256]{0,2,1:T(8,128)(2,1)S(1)} %bitcast.83, bf16[2,256,3456]{2,1,0:T(8,128)(2,1)} %all-gather.2.cloned.1.call-done, bf16[3072,128]{1,0:T(8,128)(2,1)S(1)} %copy-done), kind=kOutput, calls=%fused_computation.6 | convolution fusion | flops 403832832 | bytes 4849664 | tf_op jit(solution)/shard_map/dot_general | solution.py:25
  128.8 0.0 copy-start.4
  128.9 0.0 copy-start.2
  128.9 0.0 copy-start.3
  128.9 1.0 pad_maximum_fusion
  130.0 6.3 %all-to-all-start.5 = ((bf16[16,256,128]{2,1,0:T(8,128)(2,1)}), bf16[16,256,128]{2,1,0:T(8,128)(2,1)S(1)}, u32[]{:S(2)}, u32[]{:S(2)}) async-start(bf16[16,256,128]{2,1,0:T(8,128)(2,1)} %pad_maximum_fusion), calls=%async_computation.5 | async-start | bytes 2097152 | tf_op jit(solution)/shard_map/all_to_all | solution.py:17
  136.3 0.0 copy-done.4
  136.3 0.0 copy-done.2
  136.3 0.0 copy-done.3
  136.3 0.1 subtract_divide_fusion
  136.4 27.8 %all-to-all-done.5 = bf16[16,256,128]{2,1,0:T(8,128)(2,1)S(1)} async-done(((bf16[16,256,128]{2,1,0:T(8,128)(2,1)}), bf16[16,256,128]{2,1,0:T(8,128)(2,1)S(1)}, u32[]{:S(2)}, u32[]{:S(2)}) %all-to-all-start.5) | async-done | bytes 1048608 | tf_op jit(solution)/shard_map/all_to_all | solution.py:17
  164.3 1.3 fusion.9
  165.6 0.8 slice_bitcast_fusion.2
  (24 shorter events, 0.5 us)
Async XLA Ops:
  7.2 67.3 %all-gather.2.cloned.1.call-start = ((), (), s32[]{:S(2)}) async-start(), calls=%async_computation.6 | async-start | bytes 3760128 | tf_op jit(solution)/shard_map/all_gather | solution.py:45
  34.2 42.5 %copy-start = (bf16[3072,128]{1,0:T(8,128)(2,1)S(1)}, bf16[3072,128]{1,0:T(8,128)(2,1)}, u32[]{:S(2)}) copy-start(bf16[3072,128]{1,0:T(8,128)(2,1)} %param.7) | copy-start | bytes 2359300
  79.9 6.8 %copy-start.1 = (f32[2,256,256]{2,1,0:T(8,128)S(1)}, f32[2,256,256]{2,1,0:T(8,128)}, u32[]{:S(2)}) copy-start(f32[2,256,256]{2,1,0:T(8,128)} %param.9) | copy-start | bytes 1572868
  81.3 27.0 %all-to-all-start.3 = ((f32[32,42,128]{2,1,0:T(8,128)}), f32[32,42,128]{2,1,0:T(8,128)S(1)}, u32[]{:S(2)}, u32[]{:S(2)}) async-start(f32[32,42,128]{2,1,0:T(8,128)} %reshape.197), calls=%async_computation.3 | async-start | bytes 1572864 | tf_op jit(solution)/shard_map/all_to_all | solution.py:17
  128.8 7.4 %copy-start.4 = (f32[8]{0:T(128)S(1)}, f32[8]{0:T(128)}, u32[]{:S(2)}) copy-start(f32[8]{0:T(128)} %param.12) | copy-start | bytes 100
  128.9 7.4 %copy-start.2 = (f32[2048]{0:T(1024)S(1)}, f32[2048]{0:T(1024)}, u32[]{:S(2)}) copy-start(f32[2048]{0:T(1024)} %param.10) | copy-start | bytes 24580
  128.9 7.4 %copy-start.3 = (f32[2048]{0:T(1024)S(1)}, f32[2048]{0:T(1024)}, u32[]{:S(2)}) copy-start(f32[2048]{0:T(1024)} %param.11) | copy-start | bytes 24580
  130.0 34.3 %all-to-all-start.5 = ((bf16[16,256,128]{2,1,0:T(8,128)(2,1)}), bf16[16,256,128]{2,1,0:T(8,128)(2,1)S(1)}, u32[]{:S(2)}, u32[]{:S(2)}) async-start(bf16[16,256,128]{2,1,0:T(8,128)(2,1)} %pad_maximum_fusion), calls=%async_computation.5 | async-start | bytes 2097152 | tf_op jit(solution)/shard_map/all_to_all | solution.py:17
Sparse Core Ops, SparseCore 0:
  10.7 49.8 all-gather.1

commit v2 on v1

v2 whole, which is shorter than its diff:
```python
import jax
import jax.numpy as jnp
from jax import lax
from jax.experimental import pallas as pl
from jax.experimental.pallas import tpu as pltpu
from jax.sharding import Mesh
from jax.sharding import PartitionSpec as P

LINK = jnp.bfloat16
F32 = jnp.float32
VMEM_LIMIT = 24 * 2**20
COL = ("y", "core")
LAST = (((1,), (1,)), ((), ()))
OFFSETS = (0, -1, 1, -2, 2, -3, 3, -4)
SOON = 5
DEPTH = 768


def transfer(eigenvalues, damping, frequencies):
    detune = eigenvalues[None, :] - frequencies[:, None] * frequencies[:, None]
    width = 2.0 * damping[None, :] * frequencies[:, None] * jnp.sqrt(eigenvalues)[None, :]
    denom = detune * detune + width * width
    return (detune / denom, -width / denom)


def exchange(chunks, axis):
    return lax.all_to_all(chunks, axis, split_axis=0, concat_axis=0, tiled=True)


def spread(value, axis, count):
    return exchange(jnp.broadcast_to(value[None], (count,) + value.shape), axis)


def dot32(left, right):
    return jnp.dot(left, right, preferred_element_type=F32)


def outer32(left, right):
    return lax.dot_general(left, right, LAST, preferred_element_type=F32)


def panel(refs, index, lanes):
    parts = [ref[:, index, :, lanes] for ref in refs]
    return jnp.concatenate([p.reshape(p.shape[0] * p.shape[1], p.shape[2]) for p in parts], axis=0)


def factors_kernel(here_ref, factor_ref, out_ref):
    size = factor_ref.shape[1]
    count = len(OFFSETS)
    mine = size // (2 * count)
    core, place = here_ref[0], here_ref[1]
    square, strip = (size, size), (mine, size)
    keep = lax.broadcasted_iota(jnp.int32, square, 1) >= lax.broadcasted_iota(jnp.int32, square, 0)
    gap = lax.broadcasted_iota(jnp.int32, strip, 1) - lax.broadcasted_iota(jnp.int32, strip, 0)
    order = []
    for flip in (0, 1):
        for offset in OFFSETS:
            owner = 2 * lax.rem(place + offset + count, count) + (core if flip == 0 else 1 - core)
            order.append(jnp.where(gap == mine * owner, 1.0, 0.0))
    order = jnp.concatenate(order, axis=0).astype(jnp.bfloat16)
    for k in range(2):
        rest = jnp.where(keep, factor_ref[k], 0.0).T
        for part in range(2):
            piece = rest.astype(jnp.bfloat16)
            rest = rest - piece.astype(F32)
            out_ref[k, part] = outer32(dot32(order, piece).astype(jnp.bfloat16), order).astype(jnp.bfloat16)


def products_kernel(here_ref, *refs):
    shards, eig_ref, out_ref, tails, loads = refs[:4], refs[4], refs[5], refs[6], refs[7]
    core, place = here_ref[0], here_ref[1]
    count = len(OFFSETS)
    dofs, modes = eig_ref.shape
    cases = loads.shape[0]
    half = cases // 2
    block = dofs // (2 * count)
    behind = slice(dofs, dofs + 2 * block)
    for flip in (0, 1):
        near, far = shards[2 * flip : 2 * flip + 2]
        owner = core if flip == 0 else 1 - core
        for j, offset in enumerate(OFFSETS):
            value = near[j, :, :, behind] if j < near.shape[0] else far[j - near.shape[0], :, :, behind]
            tails[2 * lax.rem(place + offset + count, count) + owner] = value.reshape(half, 2 * block)
    for pair in range(count):
        even, odd = tails[2 * pair], tails[2 * pair + 1]
        at = slice(2 * pair * block, 2 * (pair + 1) * block)
        loads[:half, at] = jnp.concatenate([even[:, :block], odd[:, :block]], axis=1)
        loads[half:, at] = jnp.concatenate([even[:, block:], odd[:, block:]], axis=1)

    sums = cross = loaded = None
    for at in range(0, dofs, DEPTH):
        lanes = slice(at, at + DEPTH)
        first, second, case = panel(shards, 0, lanes), panel(shards, 1, lanes), loads[:, lanes]
        left = jnp.concatenate([first, second, case], axis=0)
        size = first.shape[0]
        new = dot32(left, eig_ref[lanes]), outer32(left[size:], first), outer32(case, second)
        sums, cross, loaded = new if at == 0 else (sums + new[0], cross + new[1], loaded + new[2])
    to = lambda value: value.astype(out_ref.dtype)
    rest = jnp.concatenate([cross[size:], loaded], axis=0)
    out_ref[:, :size] = to(cross[:size])
    out_ref[: size // 2, size : size + modes] = to(rest[:, :modes])
    out_ref[size // 2 :, size : size + modes] = to(rest[:, modes:])
    out_ref[:, size + modes : size + 2 * modes] = to(sums[:size])
    out_ref[:, size + 2 * modes : size + 3 * modes] = to(sums[size : 2 * size])
    out_ref[:cases, size + 3 * modes :] = to(sums[2 * size :])
    out_ref[cases:, size + 3 * modes :] = jnp.zeros((size - cases, modes), out_ref.dtype)


def rotate_kernel(total_ref, factor_ref, *refs):
    shards, eig_ref, out_ref = refs[:4], refs[4], refs[5]
    bf16 = jnp.bfloat16
    size = factor_ref.shape[2]
    dofs, modes = eig_ref.shape
    cases = size // 4
    block = out_ref.shape[1] - cases
    total = total_ref[...]
    rest = total[:, size : size + modes]
    rest = jnp.concatenate([rest[: size // 2], rest[size // 2 :]], axis=1)
    first = total[:, size + modes : size + 2 * modes]
    second = total[:, size + 2 * modes : size + 3 * modes].astype(F32)
    direct = total[:cases, size + 3 * modes :].astype(F32)
    first = (dot32(factor_ref[0, 0], first) + dot32(factor_ref[0, 1], first)).astype(bf16)
    second = second - dot32(total[:, :size], first)
    high = second.astype(bf16)
    low = (second - high.astype(F32)).astype(bf16)
    second = dot32(factor_ref[1, 0], high) + dot32(factor_ref[1, 1], high) + dot32(factor_ref[1, 0], low)
    second = second.astype(bf16)
    modal = (direct - dot32(rest[:cases], first) - dot32(rest[cases:], second)).astype(bf16)
    weights = jnp.concatenate([first, second], axis=0).T
    for at in range(0, dofs, DEPTH):
        lanes = slice(at, at + DEPTH)
        vectors = jnp.concatenate([panel(shards, 0, lanes), panel(shards, 1, lanes)], axis=0)
        rotated = (eig_ref[lanes].astype(F32) - dot32(weights, vectors).T).astype(bf16)
        for k in range(DEPTH // block):
            out_ref[at // block + k, :block] = rotated[k * block : (k + 1) * block]
            out_ref[at // block + k, block:] = modal


def gather_ring(packed, count):
    shift = [[(i, (i + s) % count) for i in range(count)] for s in (1, -1)]
    swap = [(0, 1), (1, 0)]
    held = [packed]
    up = down = packed
    for k in range(1, count // 2 + 1):
        up = lax.ppermute(up, "y", shift[0])
        held.append(up)
        if 2 * k < count:
            down = lax.ppermute(down, "y", shift[1])
            held.append(down)
    near, far = jnp.stack(held[:SOON]), jnp.stack(held[SOON:])
    return near, far, lax.ppermute(near, "core", swap), lax.ppermute(far, "core", swap)


def body(eigvectors, panel_vectors, panel_factors, eigenvalues, damping, frequencies, loads):
    rows = lax.axis_size("row")
    ys = lax.axis_size("y")
    cols = ys * 2
    bf16 = jnp.bfloat16
    _, mine, dofs = panel_vectors.shape
    modes = eigvectors.shape[1]
    cases, block = loads.shape
    size = panel_factors.shape[-1]
    width = size + 4 * modes
    here = jnp.stack([lax.axis_index("core"), lax.axis_index("y")])

    half = cases // 2
    folded = jnp.concatenate([loads[:half], loads[half:]], axis=1).reshape(2, mine, 2 * block)
    packed = jnp.concatenate([panel_vectors, folded], axis=2)
    shards = gather_ring(packed, ys)

    scalars = pl.BlockSpec(memory_space=pltpu.SMEM)
    vmem = pl.BlockSpec(memory_space=pltpu.VMEM)
    params = pltpu.CompilerParams(vmem_limit_bytes=VMEM_LIMIT)
    upper = pl.pallas_call(
        factors_kernel,
        in_specs=[scalars, vmem],
        out_specs=vmem,
        out_shape=jax.ShapeDtypeStruct((2, 2, size, size), bf16),
        compiler_params=params,
        cost_estimate=pl.CostEstimate(flops=16 * size**3, bytes_accessed=16 * size**2, transcendentals=0),
    )(here, panel_factors)
    sent = pl.pallas_call(
        products_kernel,
        in_specs=[scalars, vmem, vmem, vmem, vmem, vmem],
        out_specs=vmem,
        out_shape=jax.ShapeDtypeStruct((size, width), LINK),
        scratch_shapes=[pltpu.VMEM((cols, half, 2 * block), bf16), pltpu.VMEM((cases, dofs), bf16)],
        compiler_params=params,
    )(here, *shards, eigvectors)

    total = jnp.sum(exchange(sent.reshape(rows, size // rows, width), "row").astype(F32), axis=0)
    total = spread(total.astype(LINK), "row", rows).reshape(size, width)

    sent = pl.pallas_call(
        rotate_kernel,
        in_specs=[vmem] * 7,
        out_specs=vmem,
        out_shape=jax.ShapeDtypeStruct((cols, block + cases, modes), bf16),
        compiler_params=params,
    )(total, upper, *shards, eigvectors)
    got = exchange(sent, COL)
    all_modes = got[:, :block]
    all_modal = got[:, block:].astype(F32)

    h_real, h_imag = transfer(eigenvalues, damping, frequencies)
    count = frequencies.shape[0]
    scale = jnp.stack([h_real, h_imag]).reshape(2, count, cols, 1, modes)
    scaled = (all_modal[None, None] * scale).astype(bf16)
    product = lax.dot_general(
        scaled, all_modes, (((2, 4), (0, 2)), ((), ())), preferred_element_type=F32
    ).astype(bf16)
    return (product[0], product[1])


def solution(mesh):
    mesh = Mesh(mesh.devices.reshape(32, 8, 2), ("row", "y", "core"))
    everywhere = P(None, None, ("row", "y", "core"))
    return jax.shard_map(
        body,
        mesh=mesh,
        in_specs=(P("row", COL), P(None, COL, "row"), P(), P(), P(), P(), P(None, ("row", "y", "core"))),
        out_specs=(everywhere, everywhere),
        check_vma=False,
    )
```

time: 174 us -> 142 us (0.82)
  blocking collectives: 76.9 us -> 17.9 us
  starting transfers between devices: 11.6 us -> 61.9 us
  between operations: 14.4 us -> 0.89 us
  matrix products: 10.1 us -> 1.28 us
  waiting for transfers between devices: 49.3 us -> 41.4 us
  Pallas kernels: 0 us -> 6.11 us
    all_to_all x4 -> x1, blocking collectives: 76.9 us -> 17.9 us  [exchange(): return lax.all_to_all(chunks, axis, split_axis=0, concat_axis=0, tiled=True)]
    ppermute x0 -> x9, starting transfers between devices: none -> 43.2 us  [the longest x3 13.3 us: gather_ring(): down = lax.ppermute(down, 'y', shift[1])]
    all_to_all x2, waiting for transfers between devices: 49.2 us -> 35.5 us  [exchange(): return lax.all_to_all(chunks, axis, split_axis=0, concat_axis=0, tiled=True)]
    dot_general x9 -> x0, matrix products: 8.87 us -> none  [the longest x5 8.02 us: dot32(): lax.dot_general(left, right, (dims, ((), ())), preferred_element_type=jnp...]
    all_to_all x2, starting transfers between devices: 11.6 us -> 18.7 us  [exchange(): return lax.all_to_all(chunks, axis, split_axis=0, concat_axis=0, tiled=True)]
    pallas_call x0 -> x3, Pallas kernels: none -> 6.11 us  [the longest x1 2.55 us: body(): pl.pallas_call(products_kernel, in_specs=[scalars, vmem, vmem, vmem, vmem...]
    unnamed x12 -> x21, local copies, waits for them, and re-layouts: 0.26 us -> 6.21 us
    ppermute x0 -> x9, waiting for transfers between devices: none -> 5.92 us  [the longest x4 4.27 us: gather_ring(): up = lax.ppermute(up, 'y', shift[0])]
  transfers between devices with their start and end apart: 3 -> 11, of which waited for: 2 -> 6; matrix products, arithmetic and copies ran while one was open for 2% -> 1% of each run, Pallas kernels for 0% -> 1%
where the time goes in v2:
time: 142 us; the launch traced here: 141 us
  starting transfers between devices  61.9 us (44%)
  waiting for transfers between devices  41.4 us (29%)
  blocking collectives  17.9 us (13%)
  local copies, waits for them, and re-layouts  8.58 us (6%)
  Pallas kernels  6.11 us (4%)
  other arithmetic  3.36 us (2%)
    all_to_all x2, waiting for transfers between devices, exchange(): return lax.all_to_all(chunks, axis, split_axis=0, concat_axis=0, tiled=True)  35.5 us
    all_to_all x2, starting transfers between devices, exchange(): return lax.all_to_all(chunks, axis, split_axis=0, concat_axis=0, tiled=True)  18.7 us
    all_to_all x1, blocking collectives, exchange(): return lax.all_to_all(chunks, axis, split_axis=0, concat_axis=0, tiled=True)  17.9 us
    ppermute x3, starting transfers between devices, gather_ring(): down = lax.ppermute(down, 'y', shift[1])  13.3 us
    ppermute x1, starting transfers between devices, gather_ring(): lax.ppermute(near, 'core', swap)  12.8 us
    ppermute x4, starting transfers between devices, gather_ring(): up = lax.ppermute(up, 'y', shift[0])  9.92 us
    ppermute x1, starting transfers between devices, gather_ring(): lax.ppermute(far, 'core', swap)  7.05 us
    unnamed x21, local copies, waits for them, and re-layouts  6.21 us
  transfers between devices with their start and end apart: 11, of which 6 were waited for; matrix products, arithmetic and copies ran while one was open for 1% of the time, Pallas kernels for 1%

profile of v2, /device:TPU:1, one launch (start us, length us, event | category | flops | bytes accessed | tf_op | source)
XLA Modules:
  0.0 141.5 jit_solution(9275433431852566064)
XLA Ops:
  0.6 0.7 fusion.6
  1.4 0.1 pad_maximum_fusion.2
  1.4 0.9 pad_maximum_fusion.1
  2.4 4.0 %collective-permute-start = (bf16[2,16,3456]{2,1,0:T(8,128)(2,1)S(1)}, bf16[2,16,3456]{2,1,0:T(8,128)(2,1)S(1)}, u32[]{:S(2)}, u32[]{:S(2)}) collective-permute-start(bf16[2,16,3456]{2,1,0:T(8,128)(2,1)S(1)} %pad_maximum_fusion.1), channel_id=1, source_target_pairs={{0,2},{2,4},{4,6},{6,8},{8,10},{10,12},{12,14},{14,0},{1,3},{3,5},... | collective-permute-start | bytes 663560 | tf_op jit(solution)/shard_map/ppermute | solution.py:145
  6.4 3.8 %collective-permute-start.1 = (bf16[2,16,3456]{2,1,0:T(8,128)(2,1)S(1)}, bf16[2,16,3456]{2,1,0:T(8,128)(2,1)S(1)}, u32[]{:S(2)}, u32[]{:S(2)}) collective-permute-start(bf16[2,16,3456]{2,1,0:T(8,128)(2,1)S(1)} %pad_maximum_fusion.1), channel_id=1, source_target_pairs={{0,14},{2,0},{4,2},{6,4},{8,6},{10,8},{12,10},{14,12},{1,15},{3,1}... | collective-permute-start | bytes 663560 | tf_op jit(solution)/shard_map/ppermute | solution.py:148
  10.3 0.9 bitcast_dynamic-update-slice_fusion.4
  11.2 0.4 collective-permute-done
  11.6 2.1 %collective-permute-start.2 = (bf16[2,16,3456]{2,1,0:T(8,128)(2,1)S(1)}, bf16[2,16,3456]{2,1,0:T(8,128)(2,1)S(1)}, u32[]{:S(2)}, u32[]{:S(2)}) collective-permute-start(bf16[2,16,3456]{2,1,0:T(8,128)(2,1)S(1)} %collective-permute-done), channel_id=1, source_target_pairs={{0,2},{2,4},{4,6},{6,8},{8,10},{10,12},{12,14},{14,0},{1,3},{3,5},... | collective-permute-start | bytes 663560 | tf_op jit(solution)/shard_map/ppermute | solution.py:145
  13.7 0.0 collective-permute-done.1
  13.7 4.7 %collective-permute-start.3 = (bf16[2,16,3456]{2,1,0:T(8,128)(2,1)S(1)}, bf16[2,16,3456]{2,1,0:T(8,128)(2,1)S(1)}, u32[]{:S(2)}, u32[]{:S(2)}) collective-permute-start(bf16[2,16,3456]{2,1,0:T(8,128)(2,1)S(1)} %collective-permute-done.1), channel_id=1, source_target_pairs={{0,14},{2,0},{4,2},{6,4},{8,6},{10,8},{12,10},{14,12},{1,15},{3,1}... | collective-permute-start | bytes 663560 | tf_op jit(solution)/shard_map/ppermute | solution.py:148
  18.5 1.5 %collective-permute-done.2 = bf16[2,16,3456]{2,1,0:T(8,128)(2,1)S(1)} collective-permute-done((bf16[2,16,3456]{2,1,0:T(8,128)(2,1)S(1)}, bf16[2,16,3456]{2,1,0:T(8,128)(2,1)S(1)}, u32[]{:S(2)}, u32[]{:S(2)}) %collective-permute-start.2) | collective-permute-done | bytes 221216 | tf_op jit(solution)/shard_map/ppermute | solution.py:145
  20.0 1.9 %collective-permute-start.4 = (bf16[2,16,3456]{2,1,0:T(8,128)(2,1)S(1)}, bf16[2,16,3456]{2,1,0:T(8,128)(2,1)S(1)}, u32[]{:S(2)}, u32[]{:S(2)}) collective-permute-start(bf16[2,16,3456]{2,1,0:T(8,128)(2,1)S(1)} %collective-permute-done.2), channel_id=1, source_target_pairs={{0,2},{2,4},{4,6},{6,8},{8,10},{10,12},{12,14},{14,0},{1,3},{3,5},... | collective-permute-start | bytes 663560 | tf_op jit(solution)/shard_map/ppermute | solution.py:145
  21.9 0.0 collective-permute-done.3
  21.9 4.8 %collective-permute-start.5 = (bf16[2,16,3456]{2,1,0:T(8,128)(2,1)S(1)}, bf16[2,16,3456]{2,1,0:T(8,128)(2,1)S(1)}, u32[]{:S(2)}, u32[]{:S(2)}) collective-permute-start(bf16[2,16,3456]{2,1,0:T(8,128)(2,1)S(1)} %collective-permute-done.3), channel_id=1, source_target_pairs={{0,14},{2,0},{4,2},{6,4},{8,6},{10,8},{12,10},{14,12},{1,15},{3,1}... | collective-permute-start | bytes 663560 | tf_op jit(solution)/shard_map/ppermute | solution.py:148
  26.8 2.4 %collective-permute-done.4 = bf16[2,16,3456]{2,1,0:T(8,128)(2,1)S(1)} collective-permute-done((bf16[2,16,3456]{2,1,0:T(8,128)(2,1)S(1)}, bf16[2,16,3456]{2,1,0:T(8,128)(2,1)S(1)}, u32[]{:S(2)}, u32[]{:S(2)}) %collective-permute-start.4) | collective-permute-done | bytes 221216 | tf_op jit(solution)/shard_map/ppermute | solution.py:145
  29.1 1.9 %collective-permute-start.6 = (bf16[2,16,3456]{2,1,0:T(8,128)(2,1)S(1)}, bf16[2,16,3456]{2,1,0:T(8,128)(2,1)S(1)}, u32[]{:S(2)}, u32[]{:S(2)}) collective-permute-start(bf16[2,16,3456]{2,1,0:T(8,128)(2,1)S(1)} %collective-permute-done.4), channel_id=1, source_target_pairs={{0,2},{2,4},{4,6},{6,8},{8,10},{10,12},{12,14},{14,0},{1,3},{3,5},... | collective-permute-start | bytes 663560 | tf_op jit(solution)/shard_map/ppermute | solution.py:145
  31.1 12.8 %collective-permute-start.7 = (bf16[5,2,16,3456]{3,2,1,0:T(8,128)(2,1)S(1)}, bf16[5,2,16,3456]{3,2,1,0:T(8,128)(2,1)S(1)}, u32[]{:S(2)}, u32[]{:S(2)}) collective-permute-start(bf16[5,2,16,3456]{3,2,1,0:T(8,128)(2,1)S(1)} %bitcast_dynamic-update-slice_fusion.refs_0_), channel_id=1, source_target_pairs={{0,1},{1,0},{2,3},{3,2},{4,5},{5,4},{6,7},{7,6},{8,9},{9,8},{10,11... | collective-permute-start | bytes 3317768 | tf_op jit(solution)/shard_map/ppermute | solution.py:151
  43.9 0.0 collective-permute-done.5
  43.9 0.0 collective-permute-done.6
  43.9 0.1 pad_maximum_fusion.refs_1_
  44.0 7.0 %collective-permute-start.8 = (bf16[3,2,16,3456]{3,2,1,0:T(8,128)(2,1)S(1)}, bf16[3,2,16,3456]{3,2,1,0:T(8,128)(2,1)S(1)}, u32[]{:S(2)}, u32[]{:S(2)}) collective-permute-start(bf16[3,2,16,3456]{3,2,1,0:T(8,128)(2,1)S(1)} %pad_maximum_fusion.refs_1_), channel_id=1, source_target_pairs={{0,1},{1,0},{2,3},{3,2},{4,5},{5,4},{6,7},{7,6},{8,9},{9,8},{10,11... | collective-permute-start | bytes 1990664 | tf_op jit(solution)/shard_map/ppermute | solution.py:151
  51.1 0.1 pad_add_fusion.here_ref
  51.2 0.0 collective-permute-done.7.refs_2_
  51.2 1.6 %collective-permute-done.8.refs_3_ = bf16[3,2,16,3456]{3,2,1,0:T(8,128)(2,1)S(1)} collective-permute-done((bf16[3,2,16,3456]{3,2,1,0:T(8,128)(2,1)S(1)}, bf16[3,2,16,3456]{3,2,1,0:T(8,128)(2,1)S(1)}, u32[]{:S(2)}, u32[]{:S(2)}) %collective-permute-start.8) | collective-permute-done | bytes 663584 | tf_op jit(solution)/shard_map/ppermute | solution.py:151
  52.8 0.0 copy-start.1
  52.8 1.1 copy-done.1
  53.9 2.6 %shard_map.86 = bf16[256,768]{1,0:T(8,128)(2,1)S(1)} custom-call(s32[2]{0:T(128)S(1)} %pad_add_fusion.here_ref, bf16[5,2,16,3456]{3,2,1,0:T(8,128)(2,1)S(1)} %bitcast_dynamic-update-slice_fusion.refs_0_, bf16[3,2,16,3456]{3,2,1,0:T(8,128)(2,1)S(1)} %pad_maximum_fusion.refs_1_, bf16[5,2,16,3456]{3,2,1,0:T(8,128)(2,1)S(1)} %collective-permute-done.7.refs_2_, ...), custom_call_target="tpu_custom_call" | custom-call | tf_op jit(solution)/shard_map/pallas_call | solution.py:182
  56.5 17.9 %all_to_all.15 = bf16[32,8,768]{2,1,0:T(8,128)(2,1)} all-to-all(bf16[32,8,768]{2,1,0:T(8,128)(2,1)S(1)} %bitcast.39), channel_id=1, replica_groups=mesh['row'=32,'y'=8,'core'=2] {'row'}, dimensions={0} | all-to-all | bytes 786432 | tf_op jit(solution)/shard_map/all_to_all | solution.py:27
  74.4 1.1 reduce_sum.12
  75.5 0.8 broadcast_in_dim.2
  76.3 7.7 %all-to-all-start.1 = ((bf16[32,8,768]{2,1,0:T(8,128)(2,1)}), bf16[32,8,768]{2,1,0:T(8,128)(2,1)}, u32[]{:S(2)}, u32[]{:S(2)}) async-start(bf16[32,8,768]{2,1,0:T(8,128)(2,1)} %broadcast_in_dim.2), calls=%async_computation.1 | async-start | bytes 786432 | tf_op jit(solution)/shard_map/all_to_all | solution.py:27
  84.0 0.0 copy-start.5
  84.0 1.0 copy-done.5
  85.0 1.2 shard_map.87.factor_ref
  86.2 0.0 copy-start.3
  86.2 0.8 copy-done.3
  87.0 7.8 %all-to-all-done.1 = bf16[32,8,768]{2,1,0:T(8,128)(2,1)} async-done(((bf16[32,8,768]{2,1,0:T(8,128)(2,1)}), bf16[32,8,768]{2,1,0:T(8,128)(2,1)}, u32[]{:S(2)}, u32[]{:S(2)}) %all-to-all-start.1) | async-done | bytes 393248 | tf_op jit(solution)/shard_map/all_to_all | solution.py:27
  94.8 0.0 copy-start.2
  94.8 1.1 copy-done.2
  95.9 0.0 copy-start.4
  95.9 1.0 copy-done.4
  97.0 2.4 %shard_map.88 = bf16[16,256,128]{2,1,0:T(8,128)(2,1)S(1)} custom-call(bf16[256,768]{1,0:T(8,128)(2,1)} %bitcast.12.total_ref, bf16[2,2,256,256]{3,2,1,0:T(8,128)(2,1)S(1)} %copy-done.4, bf16[5,2,16,3456]{3,2,1,0:T(8,128)(2,1)S(1)} %bitcast_dynamic-update-slice_fusion.refs_0_, bf16[3,2,16,3456]{3,2,1,0:T(8,128)(2,1)S(1)} %pad_maximum_fusion.refs_1_, ...), custom_call_target="tpu_custom_call" | custom-call | tf_op jit(solution)/shard_map/pallas_call | solution.py:194
  99.3 0.0 copy-start
  99.4 1.0 copy-done
  100.3 0.0 copy-start.8
  100.3 0.0 copy-start.6
  100.3 0.0 copy-start.7
  100.3 11.0 %all-to-all-start.2 = ((bf16[16,256,128]{2,1,0:T(8,128)(2,1)}), bf16[16,256,128]{2,1,0:T(8,128)(2,1)S(1)}, u32[]{:S(2)}, u32[]{:S(2)}) async-start(bf16[16,256,128]{2,1,0:T(8,128)(2,1)} %copy-done), calls=%async_computation.2 | async-start | bytes 2097152 | tf_op jit(solution)/shard_map/all_to_all | solution.py:27
  111.4 0.0 copy-done.8
  111.4 0.0 copy-done.6
  111.4 0.0 copy-done.7
  111.4 0.1 subtract_divide_fusion
  111.6 27.8 %all-to-all-done.2 = bf16[16,256,128]{2,1,0:T(8,128)(2,1)S(1)} async-done(((bf16[16,256,128]{2,1,0:T(8,128)(2,1)}), bf16[16,256,128]{2,1,0:T(8,128)(2,1)S(1)}, u32[]{:S(2)}, u32[]{:S(2)}) %all-to-all-start.2) | async-done | bytes 1048608 | tf_op jit(solution)/shard_map/all_to_all | solution.py:27
  139.4 1.3 fusion.4
  140.7 0.8 slice_bitcast_fusion.2
  (8 shorter events, 0.2 us)
Async XLA Ops:
  2.4 9.2 %collective-permute-start = (bf16[2,16,3456]{2,1,0:T(8,128)(2,1)S(1)}, bf16[2,16,3456]{2,1,0:T(8,128)(2,1)S(1)}, u32[]{:S(2)}, u32[]{:S(2)}) collective-permute-start(bf16[2,16,3456]{2,1,0:T(8,128)(2,1)S(1)} %pad_maximum_fusion.1), channel_id=1, source_target_pairs={{0,2},{2,4},{4,6},{6,8},{8,10},{10,12},{12,14},{14,0},{1,3},{3,5},... | collective-permute-start | bytes 663560 | tf_op jit(solution)/shard_map/ppermute | solution.py:145
  6.4 7.3 %collective-permute-start.1 = (bf16[2,16,3456]{2,1,0:T(8,128)(2,1)S(1)}, bf16[2,16,3456]{2,1,0:T(8,128)(2,1)S(1)}, u32[]{:S(2)}, u32[]{:S(2)}) collective-permute-start(bf16[2,16,3456]{2,1,0:T(8,128)(2,1)S(1)} %pad_maximum_fusion.1), channel_id=1, source_target_pairs={{0,14},{2,0},{4,2},{6,4},{8,6},{10,8},{12,10},{14,12},{1,15},{3,1}... | collective-permute-start | bytes 663560 | tf_op jit(solution)/shard_map/ppermute | solution.py:148
  11.6 8.4 %collective-permute-start.2 = (bf16[2,16,3456]{2,1,0:T(8,128)(2,1)S(1)}, bf16[2,16,3456]{2,1,0:T(8,128)(2,1)S(1)}, u32[]{:S(2)}, u32[]{:S(2)}) collective-permute-start(bf16[2,16,3456]{2,1,0:T(8,128)(2,1)S(1)} %collective-permute-done), channel_id=1, source_target_pairs={{0,2},{2,4},{4,6},{6,8},{8,10},{10,12},{12,14},{14,0},{1,3},{3,5},... | collective-permute-start | bytes 663560 | tf_op jit(solution)/shard_map/ppermute | solution.py:145
  13.7 8.2 %collective-permute-start.3 = (bf16[2,16,3456]{2,1,0:T(8,128)(2,1)S(1)}, bf16[2,16,3456]{2,1,0:T(8,128)(2,1)S(1)}, u32[]{:S(2)}, u32[]{:S(2)}) collective-permute-start(bf16[2,16,3456]{2,1,0:T(8,128)(2,1)S(1)} %collective-permute-done.1), channel_id=1, source_target_pairs={{0,14},{2,0},{4,2},{6,4},{8,6},{10,8},{12,10},{14,12},{1,15},{3,1}... | collective-permute-start | bytes 663560 | tf_op jit(solution)/shard_map/ppermute | solution.py:148
  20.0 9.1 %collective-permute-start.4 = (bf16[2,16,3456]{2,1,0:T(8,128)(2,1)S(1)}, bf16[2,16,3456]{2,1,0:T(8,128)(2,1)S(1)}, u32[]{:S(2)}, u32[]{:S(2)}) collective-permute-start(bf16[2,16,3456]{2,1,0:T(8,128)(2,1)S(1)} %collective-permute-done.2), channel_id=1, source_target_pairs={{0,2},{2,4},{4,6},{6,8},{8,10},{10,12},{12,14},{14,0},{1,3},{3,5},... | collective-permute-start | bytes 663560 | tf_op jit(solution)/shard_map/ppermute | solution.py:145
  21.9 22.0 %collective-permute-start.5 = (bf16[2,16,3456]{2,1,0:T(8,128)(2,1)S(1)}, bf16[2,16,3456]{2,1,0:T(8,128)(2,1)S(1)}, u32[]{:S(2)}, u32[]{:S(2)}) collective-permute-start(bf16[2,16,3456]{2,1,0:T(8,128)(2,1)S(1)} %collective-permute-done.3), channel_id=1, source_target_pairs={{0,14},{2,0},{4,2},{6,4},{8,6},{10,8},{12,10},{14,12},{1,15},{3,1}... | collective-permute-start | bytes 663560 | tf_op jit(solution)/shard_map/ppermute | solution.py:148
  29.1 14.8 %collective-permute-start.6 = (bf16[2,16,3456]{2,1,0:T(8,128)(2,1)S(1)}, bf16[2,16,3456]{2,1,0:T(8,128)(2,1)S(1)}, u32[]{:S(2)}, u32[]{:S(2)}) collective-permute-start(bf16[2,16,3456]{2,1,0:T(8,128)(2,1)S(1)} %collective-permute-done.4), channel_id=1, source_target_pairs={{0,2},{2,4},{4,6},{6,8},{8,10},{10,12},{12,14},{14,0},{1,3},{3,5},... | collective-permute-start | bytes 663560 | tf_op jit(solution)/shard_map/ppermute | solution.py:145
  31.1 20.1 %collective-permute-start.7 = (bf16[5,2,16,3456]{3,2,1,0:T(8,128)(2,1)S(1)}, bf16[5,2,16,3456]{3,2,1,0:T(8,128)(2,1)S(1)}, u32[]{:S(2)}, u32[]{:S(2)}) collective-permute-start(bf16[5,2,16,3456]{3,2,1,0:T(8,128)(2,1)S(1)} %bitcast_dynamic-update-slice_fusion.refs_0_), channel_id=1, source_target_pairs={{0,1},{1,0},{2,3},{3,2},{4,5},{5,4},{6,7},{7,6},{8,9},{9,8},{10,11... | collective-permute-start | bytes 3317768 | tf_op jit(solution)/shard_map/ppermute | solution.py:151
  44.0 8.8 %collective-permute-start.8 = (bf16[3,2,16,3456]{3,2,1,0:T(8,128)(2,1)S(1)}, bf16[3,2,16,3456]{3,2,1,0:T(8,128)(2,1)S(1)}, u32[]{:S(2)}, u32[]{:S(2)}) collective-permute-start(bf16[3,2,16,3456]{3,2,1,0:T(8,128)(2,1)S(1)} %pad_maximum_fusion.refs_1_), channel_id=1, source_target_pairs={{0,1},{1,0},{2,3},{3,2},{4,5},{5,4},{6,7},{7,6},{8,9},{9,8},{10,11... | collective-permute-start | bytes 1990664 | tf_op jit(solution)/shard_map/ppermute | solution.py:151
  52.8 1.1 copy-start.1
  76.3 18.5 %all-to-all-start.1 = ((bf16[32,8,768]{2,1,0:T(8,128)(2,1)}), bf16[32,8,768]{2,1,0:T(8,128)(2,1)}, u32[]{:S(2)}, u32[]{:S(2)}) async-start(bf16[32,8,768]{2,1,0:T(8,128)(2,1)} %broadcast_in_dim.2), calls=%async_computation.1 | async-start | bytes 786432 | tf_op jit(solution)/shard_map/all_to_all | solution.py:27
  84.0 1.0 copy-start.5
  86.2 0.8 copy-start.3
  94.8 1.1 copy-start.2
  95.9 1.0 copy-start.4
  99.3 1.0 copy-start
  100.3 11.0 %copy-start.8 = (f32[8]{0:T(128)S(1)}, f32[8]{0:T(128)}, u32[]{:S(2)}) copy-start(f32[8]{0:T(128)} %param.12) | copy-start | bytes 100
  100.3 11.1 %copy-start.6 = (f32[2048]{0:T(1024)S(1)}, f32[2048]{0:T(1024)}, u32[]{:S(2)}) copy-start(f32[2048]{0:T(1024)} %param.10) | copy-start | bytes 24580
  100.3 11.1 %copy-start.7 = (f32[2048]{0:T(1024)S(1)}, f32[2048]{0:T(1024)}, u32[]{:S(2)}) copy-start(f32[2048]{0:T(1024)} %param.11) | copy-start | bytes 24580
  100.3 39.0 %all-to-all-start.2 = ((bf16[16,256,128]{2,1,0:T(8,128)(2,1)}), bf16[16,256,128]{2,1,0:T(8,128)(2,1)S(1)}, u32[]{:S(2)}, u32[]{:S(2)}) async-start(bf16[16,256,128]{2,1,0:T(8,128)(2,1)} %copy-done), calls=%async_computation.2 | async-start | bytes 2097152 | tf_op jit(solution)/shard_map/all_to_all | solution.py:27

commit v3 on v2

--- a/solution.py
+++ b/solution.py
@@ -12,8 +12,9 @@
 COL = ("y", "core")
 LAST = (((1,), (1,)), ((), ()))
 OFFSETS = (0, -1, 1, -2, 2, -3, 3, -4)
+DEPTH = 768
 SOON = 5
-DEPTH = 768
+SHARDS = 4
 
 
 def transfer(eigenvalues, damping, frequencies):
@@ -27,10 +28,6 @@
     return lax.all_to_all(chunks, axis, split_axis=0, concat_axis=0, tiled=True)
 
 
-def spread(value, axis, count):
-    return exchange(jnp.broadcast_to(value[None], (count,) + value.shape), axis)
-
-
 def dot32(left, right):
     return jnp.dot(left, right, preferred_element_type=F32)
 
@@ -42,6 +39,26 @@
 def panel(refs, index, lanes):
     parts = [ref[:, index, :, lanes] for ref in refs]
     return jnp.concatenate([p.reshape(p.shape[0] * p.shape[1], p.shape[2]) for p in parts], axis=0)
+
+
+def pack_kernel(vectors_hbm, loads_hbm, out_ref, loads_ref, sems):
+    dofs = vectors_hbm.shape[2]
+    copies = [
+        pltpu.make_async_copy(vectors_hbm, out_ref.at[:, :, :dofs], sems.at[0]),
+        pltpu.make_async_copy(loads_hbm, loads_ref, sems.at[1]),
+    ]
+    for copy in copies:
+        copy.start()
+    copies[1].wait()
+    half = loads_ref.shape[0] // 2
+    folded = jnp.concatenate([loads_ref[:half], loads_ref[half:]], axis=1)
+    out_ref[:, :, dofs:] = folded.reshape(out_ref.shape[0], out_ref.shape[1], folded.shape[1])
+    copies[0].wait()
+
+
+def sum_kernel(parts_ref, out_ref):
+    total = jnp.sum(parts_ref[...].astype(F32), axis=0).astype(out_ref.dtype)
+    out_ref[...] = jnp.broadcast_to(total[None], out_ref.shape)
 
 
 def factors_kernel(here_ref, factor_ref, out_ref):
@@ -67,7 +84,9 @@
 
 
 def products_kernel(here_ref, *refs):
-    shards, eig_ref, out_ref, tails, loads = refs[:4], refs[4], refs[5], refs[6], refs[7]
+    shards, eig_hbm, out_ref, (eig_ref, tails, loads, sem) = refs[:SHARDS], refs[SHARDS], refs[SHARDS + 1], refs[SHARDS + 2 :]
+    copy = pltpu.make_async_copy(eig_hbm, eig_ref, sem)
+    copy.start()
     core, place = here_ref[0], here_ref[1]
     count = len(OFFSETS)
     dofs, modes = eig_ref.shape
@@ -75,11 +94,11 @@
     half = cases // 2
     block = dofs // (2 * count)
     behind = slice(dofs, dofs + 2 * block)
+    blocks = [ref.at[j] for ref in shards for j in range(ref.shape[0])]
     for flip in (0, 1):
-        near, far = shards[2 * flip : 2 * flip + 2]
         owner = core if flip == 0 else 1 - core
         for j, offset in enumerate(OFFSETS):
-            value = near[j, :, :, behind] if j < near.shape[0] else far[j - near.shape[0], :, :, behind]
+            value = blocks[flip * count + j][:, :, behind]
             tails[2 * lax.rem(place + offset + count, count) + owner] = value.reshape(half, 2 * block)
     for pair in range(count):
         even, odd = tails[2 * pair], tails[2 * pair + 1]
@@ -87,14 +106,17 @@
         loads[:half, at] = jnp.concatenate([even[:, :block], odd[:, :block]], axis=1)
         loads[half:, at] = jnp.concatenate([even[:, block:], odd[:, block:]], axis=1)
 
-    sums = cross = loaded = None
+    size = out_ref.shape[0]
+    cross = loaded = sums = None
     for at in range(0, dofs, DEPTH):
         lanes = slice(at, at + DEPTH)
         first, second, case = panel(shards, 0, lanes), panel(shards, 1, lanes), loads[:, lanes]
-        left = jnp.concatenate([first, second, case], axis=0)
-        size = first.shape[0]
-        new = dot32(left, eig_ref[lanes]), outer32(left[size:], first), outer32(case, second)
-        sums, cross, loaded = new if at == 0 else (sums + new[0], cross + new[1], loaded + new[2])
+        new = outer32(jnp.concatenate([second, case], axis=0), first), outer32(case, second)
+        cross, loaded = new if at == 0 else (cross + new[0], loaded + new[1])
+        if at == 0:
+            copy.wait()
+        new = dot32(jnp.concatenate([first, second, case], axis=0), eig_ref[lanes])
+        sums = new if at == 0 else sums + new
     to = lambda value: value.astype(out_ref.dtype)
     rest = jnp.concatenate([cross[size:], loaded], axis=0)
     out_ref[:, :size] = to(cross[:size])
@@ -107,8 +129,10 @@
 
 
 def rotate_kernel(total_ref, factor_ref, *refs):
-    shards, eig_ref, out_ref = refs[:4], refs[4], refs[5]
+    shards, eig_hbm, out_hbm, (eig_ref, out_ref, eig_sem, out_sem) = refs[:SHARDS], refs[SHARDS], refs[SHARDS + 1], refs[SHARDS + 2 :]
     bf16 = jnp.bfloat16
+    eig_copy = pltpu.make_async_copy(eig_hbm, eig_ref, eig_sem)
+    eig_copy.start()
     size = factor_ref.shape[2]
     dofs, modes = eig_ref.shape
     cases = size // 4
@@ -127,6 +151,8 @@
     second = second.astype(bf16)
     modal = (direct - dot32(rest[:cases], first) - dot32(rest[cases:], second)).astype(bf16)
     weights = jnp.concatenate([first, second], axis=0).T
+    eig_copy.wait()
+    copies = []
     for at in range(0, dofs, DEPTH):
         lanes = slice(at, at + DEPTH)
         vectors = jnp.concatenate([panel(shards, 0, lanes), panel(shards, 1, lanes)], axis=0)
@@ -134,21 +160,28 @@
         for k in range(DEPTH // block):
             out_ref[at // block + k, :block] = rotated[k * block : (k + 1) * block]
             out_ref[at // block + k, block:] = modal
-
-
-def gather_ring(packed, count):
+        ready = slice(at // block, (at + DEPTH) // block)
+        copies.append(pltpu.make_async_copy(out_ref.at[ready], out_hbm.at[ready], out_sem.at[len(copies)]))
+        copies[-1].start()
+    for copy in copies:
+        copy.wait()
+
+
+def gather_ring(packed, count, upper):
     shift = [[(i, (i + s) % count) for i in range(count)] for s in (1, -1)]
-    swap = [(0, 1), (1, 0)]
+    swap = lambda blocks: lax.ppermute(blocks, "core", [(0, 1), (1, 0)])
     held = [packed]
     up = down = packed
     for k in range(1, count // 2 + 1):
         up = lax.ppermute(up, "y", shift[0])
         held.append(up)
+        if k == 2:
+            up, upper = lax.optimization_barrier((up, upper))
         if 2 * k < count:
             down = lax.ppermute(down, "y", shift[1])
             held.append(down)
     near, far = jnp.stack(held[:SOON]), jnp.stack(held[SOON:])
-    return near, far, lax.ppermute(near, "core", swap), lax.ppermute(far, "core", swap)
+    return (near, far, swap(near), swap(far)), upper
 
 
 def body(eigvectors, panel_vectors, panel_factors, eigenvalues, damping, frequencies, loads):
@@ -163,13 +196,9 @@
     width = size + 4 * modes
     here = jnp.stack([lax.axis_index("core"), lax.axis_index("y")])
 
-    half = cases // 2
-    folded = jnp.concatenate([loads[:half], loads[half:]], axis=1).reshape(2, mine, 2 * block)
-    packed = jnp.concatenate([panel_vectors, folded], axis=2)
-    shards = gather_ring(packed, ys)
-
     scalars = pl.BlockSpec(memory_space=pltpu.SMEM)
     vmem = pl.BlockSpec(memory_space=pltpu.VMEM)
+    hbm = pl.BlockSpec(memory_space=pl.ANY)
     params = pltpu.CompilerParams(vmem_limit_bytes=VMEM_LIMIT)
     upper = pl.pallas_call(
         factors_kernel,
@@ -179,23 +208,51 @@
         compiler_params=params,
         cost_estimate=pl.CostEstimate(flops=16 * size**3, bytes_accessed=16 * size**2, transcendentals=0),
     )(here, panel_factors)
+
+    packed = pl.pallas_call(
+        pack_kernel,
+        in_specs=[hbm, hbm],
+        out_specs=vmem,
+        out_shape=jax.ShapeDtypeStruct((2, mine, dofs + 2 * block), bf16),
+        scratch_shapes=[pltpu.VMEM(loads.shape, bf16), pltpu.SemaphoreType.DMA((2,))],
+        compiler_params=pltpu.CompilerParams(vmem_limit_bytes=60 * 2**20),
+    )(panel_vectors, loads)
+    shards, upper = gather_ring(packed, ys, upper)
     sent = pl.pallas_call(
         products_kernel,
-        in_specs=[scalars, vmem, vmem, vmem, vmem, vmem],
+        in_specs=[scalars] + [vmem] * SHARDS + [hbm],
         out_specs=vmem,
         out_shape=jax.ShapeDtypeStruct((size, width), LINK),
-        scratch_shapes=[pltpu.VMEM((cols, half, 2 * block), bf16), pltpu.VMEM((cases, dofs), bf16)],
+        scratch_shapes=[
+            pltpu.VMEM((dofs, modes), bf16),
+            pltpu.VMEM((cols, cases // 2, 2 * block), bf16),
+            pltpu.VMEM((cases, dofs), bf16),
+            pltpu.SemaphoreType.DMA,
+        ],
         compiler_params=params,
     )(here, *shards, eigvectors)
 
-    total = jnp.sum(exchange(sent.reshape(rows, size // rows, width), "row").astype(F32), axis=0)
-    total = spread(total.astype(LINK), "row", rows).reshape(size, width)
+    parts = exchange(sent.reshape(rows, size // rows, width), "row")
+    total = pl.pallas_call(
+        sum_kernel,
+        in_specs=[vmem],
+        out_specs=vmem,
+        out_shape=jax.ShapeDtypeStruct(parts.shape, LINK),
+        compiler_params=params,
+    )(parts)
+    total = exchange(total, "row").reshape(size, width)
 
     sent = pl.pallas_call(
         rotate_kernel,
-        in_specs=[vmem] * 7,
-        out_specs=vmem,
+        in_specs=[vmem] * (2 + SHARDS) + [hbm],
+        out_specs=hbm,
         out_shape=jax.ShapeDtypeStruct((cols, block + cases, modes), bf16),
+        scratch_shapes=[
+            pltpu.VMEM((dofs, modes), bf16),
+            pltpu.VMEM((cols, block + cases, modes), bf16),
+            pltpu.SemaphoreType.DMA,
+            pltpu.SemaphoreType.DMA((dofs // DEPTH,)),
+        ],
         compiler_params=params,
     )(total, upper, *shards, eigvectors)
     got = exchange(sent, COL)
@@ -206,9 +263,8 @@
     count = frequencies.shape[0]
     scale = jnp.stack([h_real, h_imag]).reshape(2, count, cols, 1, modes)
     scaled = (all_modal[None, None] * scale).astype(bf16)
-    product = lax.dot_general(
-        scaled, all_modes, (((2, 4), (0, 2)), ((), ())), preferred_element_type=F32
-    ).astype(bf16)
+    product = lax.dot_general(scaled, all_modes, (((2, 4), (0, 2)), ((), ())), preferred_element_type=F32)
+    product = product.astype(bf16)
     return (product[0], product[1])
 
 

time: 142 us -> 136 us (0.958)
  blocking collectives: 17.9 us -> 35.5 us
  starting transfers between devices: 61.9 us -> 53.4 us
  waiting for transfers between devices: 41.4 us -> 33.2 us
  local copies, waits for them, and re-layouts: 8.58 us -> 2.95 us
  other arithmetic: 3.36 us -> 0.33 us
  Pallas kernels: 6.11 us -> 8.04 us
    all_to_all x1 -> x2, blocking collectives: 17.9 us -> 35.5 us  [exchange(): return lax.all_to_all(chunks, axis, split_axis=0, concat_axis=0, tiled=True)]
    all_to_all x2 -> x1, waiting for transfers between devices: 35.5 us -> 27.8 us  [exchange(): return lax.all_to_all(chunks, axis, split_axis=0, concat_axis=0, tiled=True)]
    all_to_all x2 -> x1, starting transfers between devices: 18.7 us -> 11.2 us  [exchange(): return lax.all_to_all(chunks, axis, split_axis=0, concat_axis=0, tiled=True)]
    unnamed x21 -> x14, local copies, waits for them, and re-layouts: 6.21 us -> 2.1 us
    pallas_call x2 -> x4, Pallas kernels: 4.93 us -> 6.86 us  [the longest x1 2.85 us: body(): pl.pallas_call(products_kernel, in_specs=[scalars] + [vmem] * SHARDS + [h...]
  transfers between devices with their start and end apart: 11 -> 10, of which waited for: 6 -> 4; matrix products, arithmetic and copies ran while one was open for 1% -> 1% of each run, Pallas kernels for 1% -> 1%
where the time goes in v3:
time: 136 us
  starting transfers between devices  53.4 us (39%)
  blocking collectives  35.5 us (26%)
  waiting for transfers between devices  33.2 us (24%)
  Pallas kernels  8.04 us (6%)
  local copies, waits for them, and re-layouts  2.95 us (2%)
    all_to_all x2, blocking collectives, exchange(): return lax.all_to_all(chunks, axis, split_axis=0, concat_axis=0, tiled=True)  35.5 us
    all_to_all x1, waiting for transfers between devices, exchange(): return lax.all_to_all(chunks, axis, split_axis=0, concat_axis=0, tiled=True)  27.8 us
    ppermute x2, starting transfers between devices, gather_ring(): swap = lambda blocks: lax.ppermute(blocks, 'core', [(0, 1), (1, 0)])  19.4 us
    ppermute x3, starting transfers between devices, gather_ring(): down = lax.ppermute(down, 'y', shift[1])  13 us
    all_to_all x1, starting transfers between devices, exchange(): return lax.all_to_all(chunks, axis, split_axis=0, concat_axis=0, tiled=True)  11.2 us
    ppermute x4, starting transfers between devices, gather_ring(): up = lax.ppermute(up, 'y', shift[0])  9.77 us
    ppermute x4, waiting for transfers between devices, gather_ring(): up = lax.ppermute(up, 'y', shift[0])  3.69 us
    pallas_call x1, Pallas kernels, body(): pl.pallas_call(products_kernel, in_specs=[scalars] + [vmem] * SHARDS + [h...  2.85 us
  transfers between devices with their start and end apart: 10, of which 4 were waited for; matrix products, arithmetic and copies ran while one was open for 1% of the time, Pallas kernels for 1%

profile of v3, /device:TPU:1, one launch (start us, length us, event | category | flops | bytes accessed | tf_op | source)
XLA Modules:
  0.0 135.5 jit_solution(13167174395910413394)
XLA Ops:
  0.6 1.6 %shard_map.86 = bf16[2,16,3456]{2,1,0:T(8,128)(2,1)} custom-call(bf16[2,16,3072]{2,1,0:T(8,128)(2,1)} %vectors_hbm.1, bf16[64,192]{1,0:T(8,128)(2,1)} %loads_hbm.1), custom_call_target="tpu_custom_call" | custom-call | tf_op jit(solution)/shard_map/pallas_call | solution.py:212
  2.3 4.0 %collective-permute-start = (bf16[2,16,3456]{2,1,0:T(8,128)(2,1)}, bf16[2,16,3456]{2,1,0:T(8,128)(2,1)S(1)}, u32[]{:S(2)}, u32[]{:S(2)}) collective-permute-start(bf16[2,16,3456]{2,1,0:T(8,128)(2,1)} %shard_map.86), channel_id=1, source_target_pairs={{0,2},{2,4},{4,6},{6,8},{8,10},{10,12},{12,14},{14,0},{1,3},{3,5},... | collective-permute-start | bytes 663560 | tf_op jit(solution)/shard_map/ppermute | solution.py:176
  6.3 3.8 %collective-permute-start.1 = (bf16[2,16,3456]{2,1,0:T(8,128)(2,1)}, bf16[2,16,3456]{2,1,0:T(8,128)(2,1)S(1)}, u32[]{:S(2)}, u32[]{:S(2)}) collective-permute-start(bf16[2,16,3456]{2,1,0:T(8,128)(2,1)} %shard_map.86), channel_id=1, source_target_pairs={{0,14},{2,0},{4,2},{6,4},{8,6},{10,8},{12,10},{14,12},{1,15},{3,1}... | collective-permute-start | bytes 663560 | tf_op jit(solution)/shard_map/ppermute | solution.py:181
  10.1 1.0 bitcast_dynamic-update-slice_fusion.4
  11.1 0.1 pad_add_fusion.here_ref
  11.2 0.0 copy-start.1
  11.2 1.0 copy-done.1
  12.2 1.2 shard_map.87.factor_ref
  13.4 0.0 collective-permute-done
  13.4 1.9 %collective-permute-start.2 = (bf16[2,16,3456]{2,1,0:T(8,128)(2,1)S(1)}, bf16[2,16,3456]{2,1,0:T(8,128)(2,1)S(1)}, u32[]{:S(2)}, u32[]{:S(2)}) collective-permute-start(bf16[2,16,3456]{2,1,0:T(8,128)(2,1)S(1)} %collective-permute-done), channel_id=1, source_target_pairs={{0,2},{2,4},{4,6},{6,8},{8,10},{10,12},{12,14},{14,0},{1,3},{3,5},... | collective-permute-start | bytes 663560 | tf_op jit(solution)/shard_map/ppermute | solution.py:176
  15.3 0.0 collective-permute-done.1
  15.4 4.6 %collective-permute-start.3 = (bf16[2,16,3456]{2,1,0:T(8,128)(2,1)S(1)}, bf16[2,16,3456]{2,1,0:T(8,128)(2,1)S(1)}, u32[]{:S(2)}, u32[]{:S(2)}) collective-permute-start(bf16[2,16,3456]{2,1,0:T(8,128)(2,1)S(1)} %collective-permute-done.1), channel_id=1, source_target_pairs={{0,14},{2,0},{4,2},{6,4},{8,6},{10,8},{12,10},{14,12},{1,15},{3,1}... | collective-permute-start | bytes 663560 | tf_op jit(solution)/shard_map/ppermute | solution.py:181
  20.0 0.0 copy-start
  20.0 1.3 collective-permute-done.2
  21.3 1.9 %collective-permute-start.4 = (bf16[2,16,3456]{2,1,0:T(8,128)(2,1)S(1)}, bf16[2,16,3456]{2,1,0:T(8,128)(2,1)S(1)}, u32[]{:S(2)}, u32[]{:S(2)}) collective-permute-start(bf16[2,16,3456]{2,1,0:T(8,128)(2,1)S(1)} %collective-permute-done.2), channel_id=1, source_target_pairs={{0,2},{2,4},{4,6},{6,8},{8,10},{10,12},{12,14},{14,0},{1,3},{3,5},... | collective-permute-start | bytes 663560 | tf_op jit(solution)/shard_map/ppermute | solution.py:176
  23.2 0.0 collective-permute-done.3
  23.2 4.6 %collective-permute-start.5 = (bf16[2,16,3456]{2,1,0:T(8,128)(2,1)S(1)}, bf16[2,16,3456]{2,1,0:T(8,128)(2,1)S(1)}, u32[]{:S(2)}, u32[]{:S(2)}) collective-permute-start(bf16[2,16,3456]{2,1,0:T(8,128)(2,1)S(1)} %collective-permute-done.3), channel_id=1, source_target_pairs={{0,14},{2,0},{4,2},{6,4},{8,6},{10,8},{12,10},{14,12},{1,15},{3,1}... | collective-permute-start | bytes 663560 | tf_op jit(solution)/shard_map/ppermute | solution.py:181
  27.8 2.4 %collective-permute-done.4 = bf16[2,16,3456]{2,1,0:T(8,128)(2,1)S(1)} collective-permute-done((bf16[2,16,3456]{2,1,0:T(8,128)(2,1)S(1)}, bf16[2,16,3456]{2,1,0:T(8,128)(2,1)S(1)}, u32[]{:S(2)}, u32[]{:S(2)}) %collective-permute-start.4) | collective-permute-done | bytes 221216 | tf_op jit(solution)/shard_map/ppermute | solution.py:176
  30.2 1.9 %collective-permute-start.6 = (bf16[2,16,3456]{2,1,0:T(8,128)(2,1)S(1)}, bf16[2,16,3456]{2,1,0:T(8,128)(2,1)S(1)}, u32[]{:S(2)}, u32[]{:S(2)}) collective-permute-start(bf16[2,16,3456]{2,1,0:T(8,128)(2,1)S(1)} %collective-permute-done.4), channel_id=1, source_target_pairs={{0,2},{2,4},{4,6},{6,8},{8,10},{10,12},{12,14},{14,0},{1,3},{3,5},... | collective-permute-start | bytes 663560 | tf_op jit(solution)/shard_map/ppermute | solution.py:176
  32.2 12.4 %collective-permute-start.7 = (bf16[5,2,16,3456]{3,2,1,0:T(8,128)(2,1)S(1)}, bf16[5,2,16,3456]{3,2,1,0:T(8,128)(2,1)S(1)}, u32[]{:S(2)}, u32[]{:S(2)}) collective-permute-start(bf16[5,2,16,3456]{3,2,1,0:T(8,128)(2,1)S(1)} %bitcast_dynamic-update-slice_fusion.refs_0_), channel_id=1, source_target_pairs={{0,1},{1,0},{2,3},{3,2},{4,5},{5,4},{6,7},{7,6},{8,9},{9,8},{10,11... | collective-permute-start | bytes 3317768 | tf_op jit(solution)/shard_map/ppermute | solution.py:172
  44.6 0.0 collective-permute-done.5
  44.6 0.0 collective-permute-done.6
  44.6 0.1 pad_maximum_fusion.refs_1_
  44.7 7.0 %collective-permute-start.8 = (bf16[3,2,16,3456]{3,2,1,0:T(8,128)(2,1)S(1)}, bf16[3,2,16,3456]{3,2,1,0:T(8,128)(2,1)S(1)}, u32[]{:S(2)}, u32[]{:S(2)}) collective-permute-start(bf16[3,2,16,3456]{3,2,1,0:T(8,128)(2,1)S(1)} %pad_maximum_fusion.refs_1_), channel_id=1, source_target_pairs={{0,1},{1,0},{2,3},{3,2},{4,5},{5,4},{6,7},{7,6},{8,9},{9,8},{10,11... | collective-permute-start | bytes 1990664 | tf_op jit(solution)/shard_map/ppermute | solution.py:172
  51.7 1.7 %collective-permute-done.8.refs_3_ = bf16[3,2,16,3456]{3,2,1,0:T(8,128)(2,1)S(1)} collective-permute-done((bf16[3,2,16,3456]{3,2,1,0:T(8,128)(2,1)S(1)}, bf16[3,2,16,3456]{3,2,1,0:T(8,128)(2,1)S(1)}, u32[]{:S(2)}, u32[]{:S(2)}) %collective-permute-start.8) | collective-permute-done | bytes 663584 | tf_op jit(solution)/shard_map/ppermute | solution.py:172
  53.4 0.0 collective-permute-done.7.refs_2_
  53.5 0.0 copy-done
  53.5 2.8 %shard_map.88 = bf16[256,768]{1,0:T(8,128)(2,1)S(1)} custom-call(s32[2]{0:T(128)S(1)} %pad_add_fusion.here_ref, bf16[5,2,16,3456]{3,2,1,0:T(8,128)(2,1)S(1)} %bitcast_dynamic-update-slice_fusion.refs_0_, bf16[3,2,16,3456]{3,2,1,0:T(8,128)(2,1)S(1)} %pad_maximum_fusion.refs_1_, bf16[5,2,16,3456]{3,2,1,0:T(8,128)(2,1)S(1)} %collective-permute-done.7.refs_2_, ...), custom_call_target="tpu_custom_call" | custom-call | tf_op jit(solution)/shard_map/pallas_call | solution.py:221
  56.3 17.2 %all_to_all.15.parts_ref = bf16[32,8,768]{2,1,0:T(8,128)(2,1)S(1)} all-to-all(bf16[32,8,768]{2,1,0:T(8,128)(2,1)S(1)} %bitcast.39), channel_id=1, replica_groups=mesh['row'=32,'y'=8,'core'=2] {'row'}, dimensions={0} | all-to-all | bytes 786432 | tf_op jit(solution)/shard_map/all_to_all | solution.py:28
  73.5 0.1 shard_map.89
  73.6 18.2 %all_to_all.16 = bf16[32,8,768]{2,1,0:T(8,128)(2,1)S(1)} all-to-all(bf16[32,8,768]{2,1,0:T(8,128)(2,1)S(1)} %shard_map.89), channel_id=1, replica_groups=mesh['row'=32,'y'=8,'core'=2] {'row'}, dimensions={0} | all-to-all | bytes 786432 | tf_op jit(solution)/shard_map/all_to_all | solution.py:28
  91.8 2.3 %shard_map.90 = bf16[16,256,128]{2,1,0:T(8,128)(2,1)} custom-call(bf16[256,768]{1,0:T(8,128)(2,1)S(1)} %bitcast.38, bf16[2,2,256,256]{3,2,1,0:T(8,128)(2,1)S(1)} %shard_map.87.factor_ref, bf16[5,2,16,3456]{3,2,1,0:T(8,128)(2,1)S(1)} %bitcast_dynamic-update-slice_fusion.refs_0_, bf16[3,2,16,3456]{3,2,1,0:T(8,128)(2,1)S(1)} %pad_maximum_fusion.refs_1_, ...), custom_call_target="tpu_custom_call" | custom-call | tf_op jit(solution)/shard_map/pallas_call | solution.py:245
  94.2 0.0 copy-start.4
  94.2 0.0 copy-start.2
  94.2 0.0 copy-start.3
  94.2 11.2 %all-to-all-start.2 = ((bf16[16,256,128]{2,1,0:T(8,128)(2,1)}), bf16[16,256,128]{2,1,0:T(8,128)(2,1)S(1)}, u32[]{:S(2)}, u32[]{:S(2)}) async-start(bf16[16,256,128]{2,1,0:T(8,128)(2,1)} %shard_map.90), calls=%async_computation.2 | async-start | bytes 2097152 | tf_op jit(solution)/shard_map/all_to_all | solution.py:28
  105.4 0.0 copy-done.4
  105.5 0.0 copy-done.2
  105.5 0.0 copy-done.3
  105.5 0.1 subtract_divide_fusion
  105.6 27.8 %all-to-all-done.2 = bf16[16,256,128]{2,1,0:T(8,128)(2,1)S(1)} async-done(((bf16[16,256,128]{2,1,0:T(8,128)(2,1)}), bf16[16,256,128]{2,1,0:T(8,128)(2,1)S(1)}, u32[]{:S(2)}, u32[]{:S(2)}) %all-to-all-start.2) | async-done | bytes 1048608 | tf_op jit(solution)/shard_map/all_to_all | solution.py:28
  133.4 1.3 fusion.4
  134.7 0.8 slice_bitcast_fusion.2
  (8 shorter events, 0.2 us)
Async XLA Ops:
  2.3 11.1 %collective-permute-start = (bf16[2,16,3456]{2,1,0:T(8,128)(2,1)}, bf16[2,16,3456]{2,1,0:T(8,128)(2,1)S(1)}, u32[]{:S(2)}, u32[]{:S(2)}) collective-permute-start(bf16[2,16,3456]{2,1,0:T(8,128)(2,1)} %shard_map.86), channel_id=1, source_target_pairs={{0,2},{2,4},{4,6},{6,8},{8,10},{10,12},{12,14},{14,0},{1,3},{3,5},... | collective-permute-start | bytes 663560 | tf_op jit(solution)/shard_map/ppermute | solution.py:176
  6.3 9.0 %collective-permute-start.1 = (bf16[2,16,3456]{2,1,0:T(8,128)(2,1)}, bf16[2,16,3456]{2,1,0:T(8,128)(2,1)S(1)}, u32[]{:S(2)}, u32[]{:S(2)}) collective-permute-start(bf16[2,16,3456]{2,1,0:T(8,128)(2,1)} %shard_map.86), channel_id=1, source_target_pairs={{0,14},{2,0},{4,2},{6,4},{8,6},{10,8},{12,10},{14,12},{1,15},{3,1}... | collective-permute-start | bytes 663560 | tf_op jit(solution)/shard_map/ppermute | solution.py:181
  11.2 1.0 copy-start.1
  13.4 7.9 %collective-permute-start.2 = (bf16[2,16,3456]{2,1,0:T(8,128)(2,1)S(1)}, bf16[2,16,3456]{2,1,0:T(8,128)(2,1)S(1)}, u32[]{:S(2)}, u32[]{:S(2)}) collective-permute-start(bf16[2,16,3456]{2,1,0:T(8,128)(2,1)S(1)} %collective-permute-done), channel_id=1, source_target_pairs={{0,2},{2,4},{4,6},{6,8},{8,10},{10,12},{12,14},{14,0},{1,3},{3,5},... | collective-permute-start | bytes 663560 | tf_op jit(solution)/shard_map/ppermute | solution.py:176
  15.4 7.9 %collective-permute-start.3 = (bf16[2,16,3456]{2,1,0:T(8,128)(2,1)S(1)}, bf16[2,16,3456]{2,1,0:T(8,128)(2,1)S(1)}, u32[]{:S(2)}, u32[]{:S(2)}) collective-permute-start(bf16[2,16,3456]{2,1,0:T(8,128)(2,1)S(1)} %collective-permute-done.1), channel_id=1, source_target_pairs={{0,14},{2,0},{4,2},{6,4},{8,6},{10,8},{12,10},{14,12},{1,15},{3,1}... | collective-permute-start | bytes 663560 | tf_op jit(solution)/shard_map/ppermute | solution.py:181
  20.0 33.5 %copy-start = (bf16[3072,128]{1,0:T(8,128)(2,1)S(1)}, bf16[3072,128]{1,0:T(8,128)(2,1)}, u32[]{:S(2)}) copy-start(bf16[3072,128]{1,0:T(8,128)(2,1)} %refs_4_.3) | copy-start | bytes 2359300
  21.3 8.9 %collective-permute-start.4 = (bf16[2,16,3456]{2,1,0:T(8,128)(2,1)S(1)}, bf16[2,16,3456]{2,1,0:T(8,128)(2,1)S(1)}, u32[]{:S(2)}, u32[]{:S(2)}) collective-permute-start(bf16[2,16,3456]{2,1,0:T(8,128)(2,1)S(1)} %collective-permute-done.2), channel_id=1, source_target_pairs={{0,2},{2,4},{4,6},{6,8},{8,10},{10,12},{12,14},{14,0},{1,3},{3,5},... | collective-permute-start | bytes 663560 | tf_op jit(solution)/shard_map/ppermute | solution.py:176
  23.2 21.3 %collective-permute-start.5 = (bf16[2,16,3456]{2,1,0:T(8,128)(2,1)S(1)}, bf16[2,16,3456]{2,1,0:T(8,128)(2,1)S(1)}, u32[]{:S(2)}, u32[]{:S(2)}) collective-permute-start(bf16[2,16,3456]{2,1,0:T(8,128)(2,1)S(1)} %collective-permute-done.3), channel_id=1, source_target_pairs={{0,14},{2,0},{4,2},{6,4},{8,6},{10,8},{12,10},{14,12},{1,15},{3,1}... | collective-permute-start | bytes 663560 | tf_op jit(solution)/shard_map/ppermute | solution.py:181
  30.2 14.4 %collective-permute-start.6 = (bf16[2,16,3456]{2,1,0:T(8,128)(2,1)S(1)}, bf16[2,16,3456]{2,1,0:T(8,128)(2,1)S(1)}, u32[]{:S(2)}, u32[]{:S(2)}) collective-permute-start(bf16[2,16,3456]{2,1,0:T(8,128)(2,1)S(1)} %collective-permute-done.4), channel_id=1, source_target_pairs={{0,2},{2,4},{4,6},{6,8},{8,10},{10,12},{12,14},{14,0},{1,3},{3,5},... | collective-permute-start | bytes 663560 | tf_op jit(solution)/shard_map/ppermute | solution.py:176
  32.2 21.3 %collective-permute-start.7 = (bf16[5,2,16,3456]{3,2,1,0:T(8,128)(2,1)S(1)}, bf16[5,2,16,3456]{3,2,1,0:T(8,128)(2,1)S(1)}, u32[]{:S(2)}, u32[]{:S(2)}) collective-permute-start(bf16[5,2,16,3456]{3,2,1,0:T(8,128)(2,1)S(1)} %bitcast_dynamic-update-slice_fusion.refs_0_), channel_id=1, source_target_pairs={{0,1},{1,0},{2,3},{3,2},{4,5},{5,4},{6,7},{7,6},{8,9},{9,8},{10,11... | collective-permute-start | bytes 3317768 | tf_op jit(solution)/shard_map/ppermute | solution.py:172
  44.7 8.8 %collective-permute-start.8 = (bf16[3,2,16,3456]{3,2,1,0:T(8,128)(2,1)S(1)}, bf16[3,2,16,3456]{3,2,1,0:T(8,128)(2,1)S(1)}, u32[]{:S(2)}, u32[]{:S(2)}) collective-permute-start(bf16[3,2,16,3456]{3,2,1,0:T(8,128)(2,1)S(1)} %pad_maximum_fusion.refs_1_), channel_id=1, source_target_pairs={{0,1},{1,0},{2,3},{3,2},{4,5},{5,4},{6,7},{7,6},{8,9},{9,8},{10,11... | collective-permute-start | bytes 1990664 | tf_op jit(solution)/shard_map/ppermute | solution.py:172
  94.2 11.3 %copy-start.4 = (f32[8]{0:T(128)S(1)}, f32[8]{0:T(128)}, u32[]{:S(2)}) copy-start(f32[8]{0:T(128)} %param.12) | copy-start | bytes 100
  94.2 11.3 %copy-start.2 = (f32[2048]{0:T(1024)S(1)}, f32[2048]{0:T(1024)}, u32[]{:S(2)}) copy-start(f32[2048]{0:T(1024)} %param.10) | copy-start | bytes 24580
  94.2 11.3 %copy-start.3 = (f32[2048]{0:T(1024)S(1)}, f32[2048]{0:T(1024)}, u32[]{:S(2)}) copy-start(f32[2048]{0:T(1024)} %param.11) | copy-start | bytes 24580
  94.2 39.2 %all-to-all-start.2 = ((bf16[16,256,128]{2,1,0:T(8,128)(2,1)}), bf16[16,256,128]{2,1,0:T(8,128)(2,1)S(1)}, u32[]{:S(2)}, u32[]{:S(2)}) async-start(bf16[16,256,128]{2,1,0:T(8,128)(2,1)} %shard_map.90), calls=%async_computation.2 | async-start | bytes 2097152 | tf_op jit(solution)/shard_map/all_to_all | solution.py:28

commit v4 on v3

--- a/solution.py
+++ b/solution.py
@@ -111,24 +111,57 @@
     for at in range(0, dofs, DEPTH):
         lanes = slice(at, at + DEPTH)
         first, second, case = panel(shards, 0, lanes), panel(shards, 1, lanes), loads[:, lanes]
-        new = outer32(jnp.concatenate([second, case], axis=0), first), outer32(case, second)
+        own = size // 2
+        new = outer32(jnp.concatenate([second, case], axis=0), first[:own]), outer32(case, second[:own])
         cross, loaded = new if at == 0 else (cross + new[0], loaded + new[1])
         if at == 0:
             copy.wait()
         new = dot32(jnp.concatenate([first, second, case], axis=0), eig_ref[lanes])
         sums = new if at == 0 else sums + new
-    to = lambda value: value.astype(out_ref.dtype)
     rest = jnp.concatenate([cross[size:], loaded], axis=0)
-    out_ref[:, :size] = to(cross[:size])
-    out_ref[: size // 2, size : size + modes] = to(rest[:, :modes])
-    out_ref[size // 2 :, size : size + modes] = to(rest[:, modes:])
-    out_ref[:, size + modes : size + 2 * modes] = to(sums[:size])
-    out_ref[:, size + 2 * modes : size + 3 * modes] = to(sums[size : 2 * size])
-    out_ref[:cases, size + 3 * modes :] = to(sums[2 * size :])
-    out_ref[cases:, size + 3 * modes :] = jnp.zeros((size - cases, modes), out_ref.dtype)
-
-
-def rotate_kernel(total_ref, factor_ref, *refs):
+    columns = [
+        cross[:size],
+        sums[:size],
+        sums[size : 2 * size],
+        fold(rest, 2),
+        fold(sums[2 * size :], 4),
+        jnp.zeros((size, modes // 4), F32),
+    ]
+    start = 0
+    for column in columns:
+        out_ref[:, start : start + column.shape[1]] = column.astype(out_ref.dtype)
+        start += column.shape[1]
+
+
+def fold(value, count):
+    width = value.shape[1] // count
+    return jnp.concatenate([value[:, k * width : (k + 1) * width] for k in range(count)], axis=0)
+
+
+def unfold(value, count):
+    height = value.shape[0] // count
+    return jnp.concatenate([value[k * height : (k + 1) * height] for k in range(count)], axis=1)
+
+
+def first_kernel(total_ref, factor_ref, *refs):
+    shards, (weights_ref, partial_ref, applied_ref) = refs[:SHARDS], refs[SHARDS:]
+    modes = applied_ref.shape[0]
+    size = factor_ref.shape[2]
+    dofs = applied_ref.shape[1]
+    own = size // 2
+    sums = total_ref[:, modes : 2 * modes]
+    first = (dot32(factor_ref[0, 0], sums) + dot32(factor_ref[0, 1], sums)).astype(jnp.bfloat16)
+    weights_ref[...] = first
+    partial_ref[:size] = dot32(total_ref[:, :own], first[:own])
+    rest = unfold(total_ref[:, 3 * modes : 3 * modes + modes // 2], 2)
+    partial_ref[size:] = dot32(rest[: own // 2], first[:own])
+    turned = first.T
+    for at in range(0, dofs, DEPTH):
+        lanes = slice(at, at + DEPTH)
+        applied_ref[:, lanes] = dot32(turned, panel(shards, 0, lanes))
+
+
+def second_kernel(total_ref, other_ref, weights_ref, partial_ref, applied_ref, factor_ref, *refs):
     shards, eig_hbm, out_hbm, (eig_ref, out_ref, eig_sem, out_sem) = refs[:SHARDS], refs[SHARDS], refs[SHARDS + 1], refs[SHARDS + 2 :]
     bf16 = jnp.bfloat16
     eig_copy = pltpu.make_async_copy(eig_hbm, eig_ref, eig_sem)
@@ -136,27 +169,27 @@
     size = factor_ref.shape[2]
     dofs, modes = eig_ref.shape
     cases = size // 4
+    own = size // 2
     block = out_ref.shape[1] - cases
-    total = total_ref[...]
-    rest = total[:, size : size + modes]
-    rest = jnp.concatenate([rest[: size // 2], rest[size // 2 :]], axis=1)
-    first = total[:, size + modes : size + 2 * modes]
-    second = total[:, size + 2 * modes : size + 3 * modes].astype(F32)
-    direct = total[:cases, size + 3 * modes :].astype(F32)
-    first = (dot32(factor_ref[0, 0], first) + dot32(factor_ref[0, 1], first)).astype(bf16)
-    second = second - dot32(total[:, :size], first)
+    ends = slice(3 * modes, 3 * modes + modes // 2)
+    here, there = unfold(total_ref[:, ends], 2), unfold(other_ref[:, ends], 2)
+    direct = unfold(total_ref[:, ends.stop : ends.stop + modes // 4], 4).astype(F32)
+    first = weights_ref[own:]
+    cross = jnp.concatenate([other_ref[own:, :own], other_ref[:own, :own]], axis=0)
+    second = total_ref[:, 2 * modes : 3 * modes].astype(F32) - partial_ref[:size] - dot32(cross, first)
+    modal = direct - partial_ref[size:] - dot32(there[:cases], first)
     high = second.astype(bf16)
     low = (second - high.astype(F32)).astype(bf16)
     second = dot32(factor_ref[1, 0], high) + dot32(factor_ref[1, 1], high) + dot32(factor_ref[1, 0], low)
     second = second.astype(bf16)
-    modal = (direct - dot32(rest[:cases], first) - dot32(rest[cases:], second)).astype(bf16)
-    weights = jnp.concatenate([first, second], axis=0).T
+    modal = (modal - dot32(here[cases:], second[:own]) - dot32(there[cases:], second[own:])).astype(bf16)
+    turned = second.T
     eig_copy.wait()
     copies = []
     for at in range(0, dofs, DEPTH):
         lanes = slice(at, at + DEPTH)
-        vectors = jnp.concatenate([panel(shards, 0, lanes), panel(shards, 1, lanes)], axis=0)
-        rotated = (eig_ref[lanes].astype(F32) - dot32(weights, vectors).T).astype(bf16)
+        applied = applied_ref[:, lanes] + dot32(turned, panel(shards, 1, lanes))
+        rotated = (eig_ref[lanes].astype(F32) - applied.T).astype(bf16)
         for k in range(DEPTH // block):
             out_ref[at // block + k, :block] = rotated[k * block : (k + 1) * block]
             out_ref[at // block + k, block:] = modal
@@ -193,7 +226,7 @@
     modes = eigvectors.shape[1]
     cases, block = loads.shape
     size = panel_factors.shape[-1]
-    width = size + 4 * modes
+    width = 4 * modes
     here = jnp.stack([lax.axis_index("core"), lax.axis_index("y")])
 
     scalars = pl.BlockSpec(memory_space=pltpu.SMEM)
@@ -242,9 +275,22 @@
     )(parts)
     total = exchange(total, "row").reshape(size, width)
 
+    other = lax.ppermute(total, "core", [(0, 1), (1, 0)])
+    begun = pl.pallas_call(
+        first_kernel,
+        in_specs=[vmem] * (2 + SHARDS),
+        out_specs=[vmem] * 3,
+        out_shape=[
+            jax.ShapeDtypeStruct((size, modes), bf16),
+            jax.ShapeDtypeStruct((size + cases, modes), F32),
+            jax.ShapeDtypeStruct((modes, dofs), F32),
+        ],
+        compiler_params=params,
+        cost_estimate=pl.CostEstimate(flops=2 * size * modes * dofs, bytes_accessed=8 * 2**20, transcendentals=0),
+    )(total, upper, *shards)
     sent = pl.pallas_call(
-        rotate_kernel,
-        in_specs=[vmem] * (2 + SHARDS) + [hbm],
+        second_kernel,
+        in_specs=[vmem] * (6 + SHARDS) + [hbm],
         out_specs=hbm,
         out_shape=jax.ShapeDtypeStruct((cols, block + cases, modes), bf16),
         scratch_shapes=[
@@ -254,7 +300,7 @@
             pltpu.SemaphoreType.DMA((dofs // DEPTH,)),
         ],
         compiler_params=params,
-    )(total, upper, *shards, eigvectors)
+    )(total, other, *begun, upper, *shards, eigvectors)
     got = exchange(sent, COL)
     all_modes = got[:, :block]
     all_modal = got[:, block:].astype(F32)

time: 136 us -> 134 us (0.985)
  blocking collectives: 35.5 us -> 31.2 us
    ppermute x0 -> x1, starting transfers between devices: none -> 5.56 us  [body(): other = lax.ppermute(total, 'core', [(0, 1), (1, 0)])]
    all_to_all x2, blocking collectives: 35.5 us -> 31.2 us  [exchange(): return lax.all_to_all(chunks, axis, split_axis=0, concat_axis=0, tiled=True)]
    all_to_all x1, starting transfers between devices: 11.2 us -> 6.98 us  [exchange(): return lax.all_to_all(chunks, axis, split_axis=0, concat_axis=0, tiled=True)]
  transfers between devices with their start and end apart: 10 -> 11, of which waited for: 4 -> 5; matrix products, arithmetic and copies ran while one was open for 1% -> 1% of each run, Pallas kernels for 1% -> 1%
where the time goes in v4:
time: 134 us; the launch traced here: 133 us
  starting transfers between devices  54.7 us (41%)
  waiting for transfers between devices  33.7 us (25%)
  blocking collectives  31.2 us (23%)
  Pallas kernels  8.31 us (6%)
  local copies, waits for them, and re-layouts  2.95 us (2%)
    all_to_all x2, blocking collectives, exchange(): return lax.all_to_all(chunks, axis, split_axis=0, concat_axis=0, tiled=True)  31.2 us
    all_to_all x1, waiting for transfers between devices, exchange(): return lax.all_to_all(chunks, axis, split_axis=0, concat_axis=0, tiled=True)  27.8 us
    ppermute x2, starting transfers between devices, gather_ring(): swap = lambda blocks: lax.ppermute(blocks, 'core', [(0, 1), (1, 0)])  19.4 us
    ppermute x3, starting transfers between devices, gather_ring(): down = lax.ppermute(down, 'y', shift[1])  13 us
    ppermute x4, starting transfers between devices, gather_ring(): up = lax.ppermute(up, 'y', shift[0])  9.77 us
    all_to_all x1, starting transfers between devices, exchange(): return lax.all_to_all(chunks, axis, split_axis=0, concat_axis=0, tiled=True)  6.98 us
    ppermute x1, starting transfers between devices, body(): other = lax.ppermute(total, 'core', [(0, 1), (1, 0)])  5.56 us
    ppermute x4, waiting for transfers between devices, gather_ring(): up = lax.ppermute(up, 'y', shift[0])  3.69 us
  transfers between devices with their start and end apart: 11, of which 5 were waited for; matrix products, arithmetic and copies ran while one was open for 1% of the time, Pallas kernels for 1%

profile of v4, /device:TPU:1, one launch (start us, length us, event | category | flops | bytes accessed | tf_op | source)
XLA Modules:
  0.0 133.3 jit_solution(18125115531597349062)
XLA Ops:
  0.6 1.6 %shard_map.86 = bf16[2,16,3456]{2,1,0:T(8,128)(2,1)} custom-call(bf16[2,16,3072]{2,1,0:T(8,128)(2,1)} %vectors_hbm.1, bf16[64,192]{1,0:T(8,128)(2,1)} %loads_hbm.1), custom_call_target="tpu_custom_call" | custom-call | tf_op jit(solution)/shard_map/pallas_call | solution.py:245
  2.3 4.0 %collective-permute-start = (bf16[2,16,3456]{2,1,0:T(8,128)(2,1)}, bf16[2,16,3456]{2,1,0:T(8,128)(2,1)S(1)}, u32[]{:S(2)}, u32[]{:S(2)}) collective-permute-start(bf16[2,16,3456]{2,1,0:T(8,128)(2,1)} %shard_map.86), channel_id=1, source_target_pairs={{0,2},{2,4},{4,6},{6,8},{8,10},{10,12},{12,14},{14,0},{1,3},{3,5},... | collective-permute-start | bytes 663560 | tf_op jit(solution)/shard_map/ppermute | solution.py:209
  6.3 3.8 %collective-permute-start.1 = (bf16[2,16,3456]{2,1,0:T(8,128)(2,1)}, bf16[2,16,3456]{2,1,0:T(8,128)(2,1)S(1)}, u32[]{:S(2)}, u32[]{:S(2)}) collective-permute-start(bf16[2,16,3456]{2,1,0:T(8,128)(2,1)} %shard_map.86), channel_id=1, source_target_pairs={{0,14},{2,0},{4,2},{6,4},{8,6},{10,8},{12,10},{14,12},{1,15},{3,1}... | collective-permute-start | bytes 663560 | tf_op jit(solution)/shard_map/ppermute | solution.py:214
  10.1 1.0 bitcast_dynamic-update-slice_fusion.4
  11.1 0.1 pad_add_fusion.here_ref
  11.2 0.0 copy-start.1
  11.2 1.0 copy-done.1
  12.2 1.2 shard_map.87.factor_ref
  13.4 0.0 collective-permute-done
  13.4 1.9 %collective-permute-start.2 = (bf16[2,16,3456]{2,1,0:T(8,128)(2,1)S(1)}, bf16[2,16,3456]{2,1,0:T(8,128)(2,1)S(1)}, u32[]{:S(2)}, u32[]{:S(2)}) collective-permute-start(bf16[2,16,3456]{2,1,0:T(8,128)(2,1)S(1)} %collective-permute-done), channel_id=1, source_target_pairs={{0,2},{2,4},{4,6},{6,8},{8,10},{10,12},{12,14},{14,0},{1,3},{3,5},... | collective-permute-start | bytes 663560 | tf_op jit(solution)/shard_map/ppermute | solution.py:209
  15.3 0.0 collective-permute-done.1
  15.4 4.6 %collective-permute-start.3 = (bf16[2,16,3456]{2,1,0:T(8,128)(2,1)S(1)}, bf16[2,16,3456]{2,1,0:T(8,128)(2,1)S(1)}, u32[]{:S(2)}, u32[]{:S(2)}) collective-permute-start(bf16[2,16,3456]{2,1,0:T(8,128)(2,1)S(1)} %collective-permute-done.1), channel_id=1, source_target_pairs={{0,14},{2,0},{4,2},{6,4},{8,6},{10,8},{12,10},{14,12},{1,15},{3,1}... | collective-permute-start | bytes 663560 | tf_op jit(solution)/shard_map/ppermute | solution.py:214
  20.0 0.0 copy-start
  20.0 1.3 collective-permute-done.2
  21.3 1.9 %collective-permute-start.4 = (bf16[2,16,3456]{2,1,0:T(8,128)(2,1)S(1)}, bf16[2,16,3456]{2,1,0:T(8,128)(2,1)S(1)}, u32[]{:S(2)}, u32[]{:S(2)}) collective-permute-start(bf16[2,16,3456]{2,1,0:T(8,128)(2,1)S(1)} %collective-permute-done.2), channel_id=1, source_target_pairs={{0,2},{2,4},{4,6},{6,8},{8,10},{10,12},{12,14},{14,0},{1,3},{3,5},... | collective-permute-start | bytes 663560 | tf_op jit(solution)/shard_map/ppermute | solution.py:209
  23.2 0.0 collective-permute-done.3
  23.2 4.6 %collective-permute-start.5 = (bf16[2,16,3456]{2,1,0:T(8,128)(2,1)S(1)}, bf16[2,16,3456]{2,1,0:T(8,128)(2,1)S(1)}, u32[]{:S(2)}, u32[]{:S(2)}) collective-permute-start(bf16[2,16,3456]{2,1,0:T(8,128)(2,1)S(1)} %collective-permute-done.3), channel_id=1, source_target_pairs={{0,14},{2,0},{4,2},{6,4},{8,6},{10,8},{12,10},{14,12},{1,15},{3,1}... | collective-permute-start | bytes 663560 | tf_op jit(solution)/shard_map/ppermute | solution.py:214
  27.8 2.4 %collective-permute-done.4 = bf16[2,16,3456]{2,1,0:T(8,128)(2,1)S(1)} collective-permute-done((bf16[2,16,3456]{2,1,0:T(8,128)(2,1)S(1)}, bf16[2,16,3456]{2,1,0:T(8,128)(2,1)S(1)}, u32[]{:S(2)}, u32[]{:S(2)}) %collective-permute-start.4) | collective-permute-done | bytes 221216 | tf_op jit(solution)/shard_map/ppermute | solution.py:209
  30.2 1.9 %collective-permute-start.6 = (bf16[2,16,3456]{2,1,0:T(8,128)(2,1)S(1)}, bf16[2,16,3456]{2,1,0:T(8,128)(2,1)S(1)}, u32[]{:S(2)}, u32[]{:S(2)}) collective-permute-start(bf16[2,16,3456]{2,1,0:T(8,128)(2,1)S(1)} %collective-permute-done.4), channel_id=1, source_target_pairs={{0,2},{2,4},{4,6},{6,8},{8,10},{10,12},{12,14},{14,0},{1,3},{3,5},... | collective-permute-start | bytes 663560 | tf_op jit(solution)/shard_map/ppermute | solution.py:209
  32.2 12.4 %collective-permute-start.7 = (bf16[5,2,16,3456]{3,2,1,0:T(8,128)(2,1)S(1)}, bf16[5,2,16,3456]{3,2,1,0:T(8,128)(2,1)S(1)}, u32[]{:S(2)}, u32[]{:S(2)}) collective-permute-start(bf16[5,2,16,3456]{3,2,1,0:T(8,128)(2,1)S(1)} %bitcast_dynamic-update-slice_fusion.refs_0_), channel_id=1, source_target_pairs={{0,1},{1,0},{2,3},{3,2},{4,5},{5,4},{6,7},{7,6},{8,9},{9,8},{10,11... | collective-permute-start | bytes 3317768 | tf_op jit(solution)/shard_map/ppermute | solution.py:205
  44.6 0.0 collective-permute-done.5
  44.6 0.0 collective-permute-done.6
  44.6 0.1 pad_maximum_fusion.refs_1_
  44.7 7.0 %collective-permute-start.8 = (bf16[3,2,16,3456]{3,2,1,0:T(8,128)(2,1)S(1)}, bf16[3,2,16,3456]{3,2,1,0:T(8,128)(2,1)S(1)}, u32[]{:S(2)}, u32[]{:S(2)}) collective-permute-start(bf16[3,2,16,3456]{3,2,1,0:T(8,128)(2,1)S(1)} %pad_maximum_fusion.refs_1_), channel_id=1, source_target_pairs={{0,1},{1,0},{2,3},{3,2},{4,5},{5,4},{6,7},{7,6},{8,9},{9,8},{10,11... | collective-permute-start | bytes 1990664 | tf_op jit(solution)/shard_map/ppermute | solution.py:205
  51.7 1.7 %collective-permute-done.8.refs_3_ = bf16[3,2,16,3456]{3,2,1,0:T(8,128)(2,1)S(1)} collective-permute-done((bf16[3,2,16,3456]{3,2,1,0:T(8,128)(2,1)S(1)}, bf16[3,2,16,3456]{3,2,1,0:T(8,128)(2,1)S(1)}, u32[]{:S(2)}, u32[]{:S(2)}) %collective-permute-start.8) | collective-permute-done | bytes 663584 | tf_op jit(solution)/shard_map/ppermute | solution.py:205
  53.4 0.0 collective-permute-done.7.refs_2_
  53.5 0.0 copy-done
  53.5 2.8 %shard_map.88 = bf16[256,512]{1,0:T(8,128)(2,1)S(1)} custom-call(s32[2]{0:T(128)S(1)} %pad_add_fusion.here_ref, bf16[5,2,16,3456]{3,2,1,0:T(8,128)(2,1)S(1)} %bitcast_dynamic-update-slice_fusion.refs_0_, bf16[3,2,16,3456]{3,2,1,0:T(8,128)(2,1)S(1)} %pad_maximum_fusion.refs_1_, bf16[5,2,16,3456]{3,2,1,0:T(8,128)(2,1)S(1)} %collective-permute-done.7.refs_2_, ...), custom_call_target="tpu_custom_call" | custom-call | tf_op jit(solution)/shard_map/pallas_call | solution.py:254
  56.3 15.2 %all_to_all.15.parts_ref = bf16[32,8,512]{2,1,0:T(8,128)(2,1)S(1)} all-to-all(bf16[32,8,512]{2,1,0:T(8,128)(2,1)S(1)} %bitcast.41), channel_id=1, replica_groups=mesh['row'=32,'y'=8,'core'=2] {'row'}, dimensions={0} | all-to-all | bytes 524288 | tf_op jit(solution)/shard_map/all_to_all | solution.py:28
  71.4 0.1 shard_map.89
  71.5 16.0 %all_to_all.16 = bf16[32,8,512]{2,1,0:T(8,128)(2,1)S(1)} all-to-all(bf16[32,8,512]{2,1,0:T(8,128)(2,1)S(1)} %shard_map.89), channel_id=1, replica_groups=mesh['row'=32,'y'=8,'core'=2] {'row'}, dimensions={0} | all-to-all | bytes 524288 | tf_op jit(solution)/shard_map/all_to_all | solution.py:28
  87.5 5.6 %collective-permute-start.9 = (bf16[256,512]{1,0:T(8,128)(2,1)S(1)}, bf16[256,512]{1,0:T(8,128)(2,1)S(1)}, u32[]{:S(2)}, u32[]{:S(2)}) collective-permute-start(bf16[256,512]{1,0:T(8,128)(2,1)S(1)} %bitcast.38), channel_id=1, source_target_pairs={{0,1},{1,0},{2,3},{3,2},{4,5},{5,4},{6,7},{7,6},{8,9},{9,8},{10,11... | collective-permute-start | bytes 786440 | tf_op jit(solution)/shard_map/ppermute | solution.py:278
  93.1 0.6 shard_map.90
  93.7 0.5 collective-permute-done.9.other_ref
  94.2 2.0 %shard_map.91 = bf16[16,256,128]{2,1,0:T(8,128)(2,1)} custom-call(bf16[256,512]{1,0:T(8,128)(2,1)S(1)} %bitcast.40, bf16[256,512]{1,0:T(8,128)(2,1)S(1)} %collective-permute-done.9.other_ref, bf16[256,128]{1,0:T(8,128)(2,1)S(1)} %get-tuple-element.9.weights_ref, f32[320,128]{1,0:T(8,128)S(1)} %get-tuple-element.10.partial_ref, ...), custom_call_target="tpu_custom_call" | custom-call | tf_op jit(solution)/shard_map/pallas_call | solution.py:291
  96.2 0.0 copy-start.4
  96.2 0.0 copy-start.2
  96.3 0.0 copy-start.3
  96.3 7.0 %all-to-all-start.2 = ((bf16[16,256,128]{2,1,0:T(8,128)(2,1)}), bf16[16,256,128]{2,1,0:T(8,128)(2,1)S(1)}, u32[]{:S(2)}, u32[]{:S(2)}) async-start(bf16[16,256,128]{2,1,0:T(8,128)(2,1)} %shard_map.91), calls=%async_computation.2 | async-start | bytes 2097152 | tf_op jit(solution)/shard_map/all_to_all | solution.py:28
  103.3 0.0 copy-done.4
  103.3 0.0 copy-done.2
  103.3 0.0 copy-done.3
  103.3 0.1 subtract_divide_fusion
  103.4 27.8 %all-to-all-done.2 = bf16[16,256,128]{2,1,0:T(8,128)(2,1)S(1)} async-done(((bf16[16,256,128]{2,1,0:T(8,128)(2,1)}), bf16[16,256,128]{2,1,0:T(8,128)(2,1)S(1)}, u32[]{:S(2)}, u32[]{:S(2)}) %all-to-all-start.2) | async-done | bytes 1048608 | tf_op jit(solution)/shard_map/all_to_all | solution.py:28
  131.2 1.3 fusion.4
  132.5 0.8 slice_bitcast_fusion.2
  (8 shorter events, 0.2 us)
Async XLA Ops:
  2.3 11.1 %collective-permute-start = (bf16[2,16,3456]{2,1,0:T(8,128)(2,1)}, bf16[2,16,3456]{2,1,0:T(8,128)(2,1)S(1)}, u32[]{:S(2)}, u32[]{:S(2)}) collective-permute-start(bf16[2,16,3456]{2,1,0:T(8,128)(2,1)} %shard_map.86), channel_id=1, source_target_pairs={{0,2},{2,4},{4,6},{6,8},{8,10},{10,12},{12,14},{14,0},{1,3},{3,5},... | collective-permute-start | bytes 663560 | tf_op jit(solution)/shard_map/ppermute | solution.py:209
  6.3 9.0 %collective-permute-start.1 = (bf16[2,16,3456]{2,1,0:T(8,128)(2,1)}, bf16[2,16,3456]{2,1,0:T(8,128)(2,1)S(1)}, u32[]{:S(2)}, u32[]{:S(2)}) collective-permute-start(bf16[2,16,3456]{2,1,0:T(8,128)(2,1)} %shard_map.86), channel_id=1, source_target_pairs={{0,14},{2,0},{4,2},{6,4},{8,6},{10,8},{12,10},{14,12},{1,15},{3,1}... | collective-permute-start | bytes 663560 | tf_op jit(solution)/shard_map/ppermute | solution.py:214
  11.2 1.0 copy-start.1
  13.4 7.9 %collective-permute-start.2 = (bf16[2,16,3456]{2,1,0:T(8,128)(2,1)S(1)}, bf16[2,16,3456]{2,1,0:T(8,128)(2,1)S(1)}, u32[]{:S(2)}, u32[]{:S(2)}) collective-permute-start(bf16[2,16,3456]{2,1,0:T(8,128)(2,1)S(1)} %collective-permute-done), channel_id=1, source_target_pairs={{0,2},{2,4},{4,6},{6,8},{8,10},{10,12},{12,14},{14,0},{1,3},{3,5},... | collective-permute-start | bytes 663560 | tf_op jit(solution)/shard_map/ppermute | solution.py:209
  15.4 7.9 %collective-permute-start.3 = (bf16[2,16,3456]{2,1,0:T(8,128)(2,1)S(1)}, bf16[2,16,3456]{2,1,0:T(8,128)(2,1)S(1)}, u32[]{:S(2)}, u32[]{:S(2)}) collective-permute-start(bf16[2,16,3456]{2,1,0:T(8,128)(2,1)S(1)} %collective-permute-done.1), channel_id=1, source_target_pairs={{0,14},{2,0},{4,2},{6,4},{8,6},{10,8},{12,10},{14,12},{1,15},{3,1}... | collective-permute-start | bytes 663560 | tf_op jit(solution)/shard_map/ppermute | solution.py:214
  20.0 33.5 %copy-start = (bf16[3072,128]{1,0:T(8,128)(2,1)S(1)}, bf16[3072,128]{1,0:T(8,128)(2,1)}, u32[]{:S(2)}) copy-start(bf16[3072,128]{1,0:T(8,128)(2,1)} %refs_4_.3) | copy-start | bytes 2359300
  21.3 8.9 %collective-permute-start.4 = (bf16[2,16,3456]{2,1,0:T(8,128)(2,1)S(1)}, bf16[2,16,3456]{2,1,0:T(8,128)(2,1)S(1)}, u32[]{:S(2)}, u32[]{:S(2)}) collective-permute-start(bf16[2,16,3456]{2,1,0:T(8,128)(2,1)S(1)} %collective-permute-done.2), channel_id=1, source_target_pairs={{0,2},{2,4},{4,6},{6,8},{8,10},{10,12},{12,14},{14,0},{1,3},{3,5},... | collective-permute-start | bytes 663560 | tf_op jit(solution)/shard_map/ppermute | solution.py:209
  23.2 21.3 %collective-permute-start.5 = (bf16[2,16,3456]{2,1,0:T(8,128)(2,1)S(1)}, bf16[2,16,3456]{2,1,0:T(8,128)(2,1)S(1)}, u32[]{:S(2)}, u32[]{:S(2)}) collective-permute-start(bf16[2,16,3456]{2,1,0:T(8,128)(2,1)S(1)} %collective-permute-done.3), channel_id=1, source_target_pairs={{0,14},{2,0},{4,2},{6,4},{8,6},{10,8},{12,10},{14,12},{1,15},{3,1}... | collective-permute-start | bytes 663560 | tf_op jit(solution)/shard_map/ppermute | solution.py:214
  30.2 14.4 %collective-permute-start.6 = (bf16[2,16,3456]{2,1,0:T(8,128)(2,1)S(1)}, bf16[2,16,3456]{2,1,0:T(8,128)(2,1)S(1)}, u32[]{:S(2)}, u32[]{:S(2)}) collective-permute-start(bf16[2,16,3456]{2,1,0:T(8,128)(2,1)S(1)} %collective-permute-done.4), channel_id=1, source_target_pairs={{0,2},{2,4},{4,6},{6,8},{8,10},{10,12},{12,14},{14,0},{1,3},{3,5},... | collective-permute-start | bytes 663560 | tf_op jit(solution)/shard_map/ppermute | solution.py:209
  32.2 21.3 %collective-permute-start.7 = (bf16[5,2,16,3456]{3,2,1,0:T(8,128)(2,1)S(1)}, bf16[5,2,16,3456]{3,2,1,0:T(8,128)(2,1)S(1)}, u32[]{:S(2)}, u32[]{:S(2)}) collective-permute-start(bf16[5,2,16,3456]{3,2,1,0:T(8,128)(2,1)S(1)} %bitcast_dynamic-update-slice_fusion.refs_0_), channel_id=1, source_target_pairs={{0,1},{1,0},{2,3},{3,2},{4,5},{5,4},{6,7},{7,6},{8,9},{9,8},{10,11... | collective-permute-start | bytes 3317768 | tf_op jit(solution)/shard_map/ppermute | solution.py:205
  44.7 8.8 %collective-permute-start.8 = (bf16[3,2,16,3456]{3,2,1,0:T(8,128)(2,1)S(1)}, bf16[3,2,16,3456]{3,2,1,0:T(8,128)(2,1)S(1)}, u32[]{:S(2)}, u32[]{:S(2)}) collective-permute-start(bf16[3,2,16,3456]{3,2,1,0:T(8,128)(2,1)S(1)} %pad_maximum_fusion.refs_1_), channel_id=1, source_target_pairs={{0,1},{1,0},{2,3},{3,2},{4,5},{5,4},{6,7},{7,6},{8,9},{9,8},{10,11... | collective-permute-start | bytes 1990664 | tf_op jit(solution)/shard_map/ppermute | solution.py:205
  87.5 6.7 %collective-permute-start.9 = (bf16[256,512]{1,0:T(8,128)(2,1)S(1)}, bf16[256,512]{1,0:T(8,128)(2,1)S(1)}, u32[]{:S(2)}, u32[]{:S(2)}) collective-permute-start(bf16[256,512]{1,0:T(8,128)(2,1)S(1)} %bitcast.38), channel_id=1, source_target_pairs={{0,1},{1,0},{2,3},{3,2},{4,5},{5,4},{6,7},{7,6},{8,9},{9,8},{10,11... | collective-permute-start | bytes 786440 | tf_op jit(solution)/shard_map/ppermute | solution.py:278
  96.2 7.0 %copy-start.4 = (f32[8]{0:T(128)S(1)}, f32[8]{0:T(128)}, u32[]{:S(2)}) copy-start(f32[8]{0:T(128)} %param.12) | copy-start | bytes 100
  96.2 7.0 %copy-start.2 = (f32[2048]{0:T(1024)S(1)}, f32[2048]{0:T(1024)}, u32[]{:S(2)}) copy-start(f32[2048]{0:T(1024)} %param.10) | copy-start | bytes 24580
  96.3 7.0 %copy-start.3 = (f32[2048]{0:T(1024)S(1)}, f32[2048]{0:T(1024)}, u32[]{:S(2)}) copy-start(f32[2048]{0:T(1024)} %param.11) | copy-start | bytes 24580
  96.3 34.9 %all-to-all-start.2 = ((bf16[16,256,128]{2,1,0:T(8,128)(2,1)}), bf16[16,256,128]{2,1,0:T(8,128)(2,1)S(1)}, u32[]{:S(2)}, u32[]{:S(2)}) async-start(bf16[16,256,128]{2,1,0:T(8,128)(2,1)} %shard_map.91), calls=%async_computation.2 | async-start | bytes 2097152 | tf_op jit(solution)/shard_map/all_to_all | solution.py:28

commit v5 on v4

--- a/solution.py
+++ b/solution.py
@@ -83,54 +83,66 @@
             out_ref[k, part] = outer32(dot32(order, piece).astype(jnp.bfloat16), order).astype(jnp.bfloat16)
 
 
-def products_kernel(here_ref, *refs):
-    shards, eig_hbm, out_ref, (eig_ref, tails, loads, sem) = refs[:SHARDS], refs[SHARDS], refs[SHARDS + 1], refs[SHARDS + 2 :]
+def place_loads(here_ref, shards, flip, tails, loads):
+    core, place = here_ref[0], here_ref[1]
+    count = len(OFFSETS)
+    cases, dofs = loads.shape
+    half, block = cases // 2, dofs // (2 * count)
+    blocks = [ref.at[j] for ref in shards for j in range(ref.shape[0])]
+    for j, offset in enumerate(OFFSETS):
+        tails[lax.rem(place + offset + count, count)] = blocks[j][:, :, dofs : dofs + 2 * block].reshape(half, 2 * block)
+    even = core == flip
+    for pair in range(count):
+        value = tails[pair]
+        left, right = jnp.where(even, value, 0), jnp.where(even, 0, value)
+        at = slice(2 * pair * block, 2 * (pair + 1) * block)
+        loads[:half, at] = jnp.concatenate([left[:, :block], right[:, :block]], axis=1)
+        loads[half:, at] = jnp.concatenate([left[:, block:], right[:, block:]], axis=1)
+
+
+def accumulate(own, shards, loads, eig_ref, copy):
+    gram = sums = None
+    for at in range(0, eig_ref.shape[0], DEPTH):
+        lanes = slice(at, at + DEPTH)
+        first, second, case = panel(shards, 0, lanes), panel(shards, 1, lanes), loads[:, lanes]
+        mine = (first, second) if own is shards else (panel(own, 0, lanes), panel(own, 1, lanes))
+        left = jnp.concatenate([second, case], axis=0)
+        new = jnp.concatenate([outer32(left, mine[0]), outer32(case, mine[1])], axis=0)
+        gram = new if at == 0 else gram + new
+        if at == 0 and copy is not None:
+            copy.wait()
+        new = dot32(jnp.concatenate([first, left], axis=0), eig_ref[lanes])
+        sums = new if at == 0 else sums + new
+    return sums, gram
+
+
+def own_kernel(here_ref, near, far, eig_hbm, sums_ref, gram_ref, eig_ref, tails, loads, sem):
     copy = pltpu.make_async_copy(eig_hbm, eig_ref, sem)
     copy.start()
-    core, place = here_ref[0], here_ref[1]
-    count = len(OFFSETS)
-    dofs, modes = eig_ref.shape
-    cases = loads.shape[0]
-    half = cases // 2
-    block = dofs // (2 * count)
-    behind = slice(dofs, dofs + 2 * block)
-    blocks = [ref.at[j] for ref in shards for j in range(ref.shape[0])]
-    for flip in (0, 1):
-        owner = core if flip == 0 else 1 - core
-        for j, offset in enumerate(OFFSETS):
-            value = blocks[flip * count + j][:, :, behind]
-            tails[2 * lax.rem(place + offset + count, count) + owner] = value.reshape(half, 2 * block)
-    for pair in range(count):
-        even, odd = tails[2 * pair], tails[2 * pair + 1]
-        at = slice(2 * pair * block, 2 * (pair + 1) * block)
-        loads[:half, at] = jnp.concatenate([even[:, :block], odd[:, :block]], axis=1)
-        loads[half:, at] = jnp.concatenate([even[:, block:], odd[:, block:]], axis=1)
-
-    size = out_ref.shape[0]
-    cross = loaded = sums = None
-    for at in range(0, dofs, DEPTH):
-        lanes = slice(at, at + DEPTH)
-        first, second, case = panel(shards, 0, lanes), panel(shards, 1, lanes), loads[:, lanes]
-        own = size // 2
-        new = outer32(jnp.concatenate([second, case], axis=0), first[:own]), outer32(case, second[:own])
-        cross, loaded = new if at == 0 else (cross + new[0], loaded + new[1])
-        if at == 0:
-            copy.wait()
-        new = dot32(jnp.concatenate([first, second, case], axis=0), eig_ref[lanes])
-        sums = new if at == 0 else sums + new
-    rest = jnp.concatenate([cross[size:], loaded], axis=0)
-    columns = [
-        cross[:size],
-        sums[:size],
-        sums[size : 2 * size],
-        fold(rest, 2),
-        fold(sums[2 * size :], 4),
-        jnp.zeros((size, modes // 4), F32),
-    ]
-    start = 0
-    for column in columns:
-        out_ref[:, start : start + column.shape[1]] = column.astype(out_ref.dtype)
-        start += column.shape[1]
+    shards = (near, far)
+    place_loads(here_ref, shards, 0, tails, loads)
+    sums_ref[...], gram_ref[...] = accumulate(shards, shards, loads, eig_ref, copy)
+
+
+def other_kernel(here_ref, near, far, other_near, other_far, sums_ref, gram_ref, eig_ref, out_ref, tails, loads):
+    shards = (other_near, other_far)
+    place_loads(here_ref, shards, 1, tails, loads)
+    sums, gram = accumulate((near, far), shards, loads, eig_ref, None)
+    size, modes = out_ref.shape[0], eig_ref.shape[1]
+    own = size // 2
+    to = lambda value: value.astype(out_ref.dtype)
+    out_ref[:own, :own] = to(gram_ref[:own])
+    out_ref[own:, :own] = to(gram[:own])
+    for k in range(2):
+        at = slice(own + k * modes, own + (k + 1) * modes)
+        out_ref[:own, at] = to(sums_ref[k * own : (k + 1) * own])
+        out_ref[own:, at] = to(sums[k * own : (k + 1) * own])
+    start = own + 2 * modes
+    for value, count in ((gram_ref[own:] + gram[own:], 2), (sums_ref[size:] + sums[size:], 4)):
+        value = fold(value, count)
+        out_ref[:, start : start + value.shape[1]] = to(value)
+        start += value.shape[1]
+    out_ref[:, start:] = jnp.zeros((size, out_ref.shape[1] - start), out_ref.dtype)
 
 
 def fold(value, count):
@@ -162,10 +174,8 @@
 
 
 def second_kernel(total_ref, other_ref, weights_ref, partial_ref, applied_ref, factor_ref, *refs):
-    shards, eig_hbm, out_hbm, (eig_ref, out_ref, eig_sem, out_sem) = refs[:SHARDS], refs[SHARDS], refs[SHARDS + 1], refs[SHARDS + 2 :]
+    shards, eig_ref, out_hbm, (out_ref, out_sem) = refs[:SHARDS], refs[SHARDS], refs[SHARDS + 1], refs[SHARDS + 2 :]
     bf16 = jnp.bfloat16
-    eig_copy = pltpu.make_async_copy(eig_hbm, eig_ref, eig_sem)
-    eig_copy.start()
     size = factor_ref.shape[2]
     dofs, modes = eig_ref.shape
     cases = size // 4
@@ -184,7 +194,6 @@
     second = second.astype(bf16)
     modal = (modal - dot32(here[cases:], second[:own]) - dot32(there[cases:], second[own:])).astype(bf16)
     turned = second.T
-    eig_copy.wait()
     copies = []
     for at in range(0, dofs, DEPTH):
         lanes = slice(at, at + DEPTH)
@@ -232,6 +241,7 @@
     scalars = pl.BlockSpec(memory_space=pltpu.SMEM)
     vmem = pl.BlockSpec(memory_space=pltpu.VMEM)
     hbm = pl.BlockSpec(memory_space=pl.ANY)
+    far_memory = pl.BlockSpec(memory_space=pltpu.HBM)
     params = pltpu.CompilerParams(vmem_limit_bytes=VMEM_LIMIT)
     upper = pl.pallas_call(
         factors_kernel,
@@ -244,26 +254,40 @@
 
     packed = pl.pallas_call(
         pack_kernel,
-        in_specs=[hbm, hbm],
+        in_specs=[far_memory, far_memory],
         out_specs=vmem,
         out_shape=jax.ShapeDtypeStruct((2, mine, dofs + 2 * block), bf16),
         scratch_shapes=[pltpu.VMEM(loads.shape, bf16), pltpu.SemaphoreType.DMA((2,))],
-        compiler_params=pltpu.CompilerParams(vmem_limit_bytes=60 * 2**20),
+        compiler_params=params,
     )(panel_vectors, loads)
     shards, upper = gather_ring(packed, ys, upper)
+    own = size // 2
+    scratch = [
+        pltpu.VMEM((ys, cases // 2, 2 * block), bf16),
+        pltpu.VMEM((cases, dofs), bf16),
+    ]
+    begun = pl.pallas_call(
+        own_kernel,
+        in_specs=[scalars, vmem, vmem, hbm],
+        out_specs=[vmem] * 3,
+        out_shape=[
+            jax.ShapeDtypeStruct((size + cases, modes), F32),
+            jax.ShapeDtypeStruct((own + 2 * cases, own), F32),
+            jax.ShapeDtypeStruct(eigvectors.shape, bf16),
+        ],
+        scratch_shapes=[*scratch, pltpu.SemaphoreType.DMA],
+        compiler_params=params,
+        cost_estimate=pl.CostEstimate(flops=4 * size * modes * dofs, bytes_accessed=4 * 2**20, transcendentals=0),
+    )(here, *shards[:2], eigvectors)
     sent = pl.pallas_call(
-        products_kernel,
-        in_specs=[scalars] + [vmem] * SHARDS + [hbm],
+        other_kernel,
+        in_specs=[scalars] + [vmem] * (SHARDS + 3),
         out_specs=vmem,
         out_shape=jax.ShapeDtypeStruct((size, width), LINK),
-        scratch_shapes=[
-            pltpu.VMEM((dofs, modes), bf16),
-            pltpu.VMEM((cols, cases // 2, 2 * block), bf16),
-            pltpu.VMEM((cases, dofs), bf16),
-            pltpu.SemaphoreType.DMA,
-        ],
-        compiler_params=params,
-    )(here, *shards, eigvectors)
+        scratch_shapes=scratch,
+        compiler_params=params,
+    )(here, *shards, *begun)
+    eigvectors = begun[2]
 
     parts = exchange(sent.reshape(rows, size // rows, width), "row")
     total = pl.pallas_call(
@@ -290,13 +314,11 @@
     )(total, upper, *shards)
     sent = pl.pallas_call(
         second_kernel,
-        in_specs=[vmem] * (6 + SHARDS) + [hbm],
+        in_specs=[vmem] * (7 + SHARDS),
         out_specs=hbm,
         out_shape=jax.ShapeDtypeStruct((cols, block + cases, modes), bf16),
         scratch_shapes=[
-            pltpu.VMEM((dofs, modes), bf16),
             pltpu.VMEM((cols, block + cases, modes), bf16),
-            pltpu.SemaphoreType.DMA,
             pltpu.SemaphoreType.DMA((dofs // DEPTH,)),
         ],
         compiler_params=params,

time: 134 us -> 134 us (level)
  waiting for transfers between devices: 33.7 us -> 32 us
    ppermute x2, waiting for transfers between devices: 1.72 us -> 0.01 us  [gather_ring(): swap = lambda blocks: lax.ppermute(blocks, 'core', [(0, 1), (1, 0)])]
    unnamed x14 -> x18, local copies, waits for them, and re-layouts: 2.1 us -> 2.83 us
    pallas_call x3 -> x4, Pallas kernels: 6.47 us -> 6.03 us  [the longest x1 2.02 us: body(): pl.pallas_call(other_kernel, in_specs=[scalars] + [vmem] * (SHARDS + 3),...]
  transfers between devices with their start and end apart: 11 -> 11, of which waited for: 5 -> 4; matrix products, arithmetic and copies ran while one was open for 1% -> 0% of each run, Pallas kernels for 1% -> 3%
where the time goes in v5:
time: 134 us; the launch traced here: 133 us
  starting transfers between devices  54.5 us (41%)
  blocking collectives  32.4 us (24%)
  waiting for transfers between devices  32 us (24%)
  Pallas kernels  7.87 us (6%)
  local copies, waits for them, and re-layouts  3.68 us (3%)
    all_to_all x2, blocking collectives, exchange(): return lax.all_to_all(chunks, axis, split_axis=0, concat_axis=0, tiled=True)  32.4 us
    all_to_all x1, waiting for transfers between devices, exchange(): return lax.all_to_all(chunks, axis, split_axis=0, concat_axis=0, tiled=True)  27.8 us
    ppermute x2, starting transfers between devices, gather_ring(): swap = lambda blocks: lax.ppermute(blocks, 'core', [(0, 1), (1, 0)])  19.4 us
    ppermute x3, starting transfers between devices, gather_ring(): down = lax.ppermute(down, 'y', shift[1])  13 us
    ppermute x4, starting transfers between devices, gather_ring(): up = lax.ppermute(up, 'y', shift[0])  9.77 us
    all_to_all x1, starting transfers between devices, exchange(): return lax.all_to_all(chunks, axis, split_axis=0, concat_axis=0, tiled=True)  6.79 us
    ppermute x1, starting transfers between devices, body(): other = lax.ppermute(total, 'core', [(0, 1), (1, 0)])  5.51 us
    ppermute x4, waiting for transfers between devices, gather_ring(): up = lax.ppermute(up, 'y', shift[0])  3.68 us
  transfers between devices with their start and end apart: 11, of which 4 were waited for; matrix products, arithmetic and copies ran while one was open for 0% of the time, Pallas kernels for 3%

profile of v5, /device:TPU:1, one launch (start us, length us, event | category | flops | bytes accessed | tf_op | source)
XLA Modules:
  0.0 133.0 jit_solution(8279591789290745929)
XLA Ops:
  0.6 0.0 copy-start.2
  0.6 0.9 copy-done.2
  1.6 0.0 copy-start.3
  1.6 0.8 copy-done.3
  2.3 0.2 shard_map.86
  2.5 4.0 %collective-permute-start = (bf16[2,16,3456]{2,1,0:T(8,128)(2,1)S(1)}, bf16[2,16,3456]{2,1,0:T(8,128)(2,1)S(1)}, u32[]{:S(2)}, u32[]{:S(2)}) collective-permute-start(bf16[2,16,3456]{2,1,0:T(8,128)(2,1)S(1)} %shard_map.86), channel_id=1, source_target_pairs={{0,2},{2,4},{4,6},{6,8},{8,10},{10,12},{12,14},{14,0},{1,3},{3,5},... | collective-permute-start | bytes 663560 | tf_op jit(solution)/shard_map/ppermute | solution.py:218
  6.6 3.8 %collective-permute-start.1 = (bf16[2,16,3456]{2,1,0:T(8,128)(2,1)S(1)}, bf16[2,16,3456]{2,1,0:T(8,128)(2,1)S(1)}, u32[]{:S(2)}, u32[]{:S(2)}) collective-permute-start(bf16[2,16,3456]{2,1,0:T(8,128)(2,1)S(1)} %shard_map.86), channel_id=1, source_target_pairs={{0,14},{2,0},{4,2},{6,4},{8,6},{10,8},{12,10},{14,12},{1,15},{3,1}... | collective-permute-start | bytes 663560 | tf_op jit(solution)/shard_map/ppermute | solution.py:223
  10.4 0.1 pad_add_fusion.here_ref
  10.5 0.0 copy-start.1
  10.5 1.0 copy-done.1
  11.5 1.2 shard_map.87.factor_ref
  12.7 0.0 collective-permute-done
  12.7 1.9 %collective-permute-start.2 = (bf16[2,16,3456]{2,1,0:T(8,128)(2,1)S(1)}, bf16[2,16,3456]{2,1,0:T(8,128)(2,1)S(1)}, u32[]{:S(2)}, u32[]{:S(2)}) collective-permute-start(bf16[2,16,3456]{2,1,0:T(8,128)(2,1)S(1)} %collective-permute-done), channel_id=1, source_target_pairs={{0,2},{2,4},{4,6},{6,8},{8,10},{10,12},{12,14},{14,0},{1,3},{3,5},... | collective-permute-start | bytes 663560 | tf_op jit(solution)/shard_map/ppermute | solution.py:218
  14.6 0.0 collective-permute-done.1
  14.7 4.6 %collective-permute-start.3 = (bf16[2,16,3456]{2,1,0:T(8,128)(2,1)S(1)}, bf16[2,16,3456]{2,1,0:T(8,128)(2,1)S(1)}, u32[]{:S(2)}, u32[]{:S(2)}) collective-permute-start(bf16[2,16,3456]{2,1,0:T(8,128)(2,1)S(1)} %collective-permute-done.1), channel_id=1, source_target_pairs={{0,14},{2,0},{4,2},{6,4},{8,6},{10,8},{12,10},{14,12},{1,15},{3,1}... | collective-permute-start | bytes 663560 | tf_op jit(solution)/shard_map/ppermute | solution.py:223
  19.3 0.0 copy-start
  19.3 1.3 collective-permute-done.2
  20.6 1.9 %collective-permute-start.4 = (bf16[2,16,3456]{2,1,0:T(8,128)(2,1)S(1)}, bf16[2,16,3456]{2,1,0:T(8,128)(2,1)S(1)}, u32[]{:S(2)}, u32[]{:S(2)}) collective-permute-start(bf16[2,16,3456]{2,1,0:T(8,128)(2,1)S(1)} %collective-permute-done.2), channel_id=1, source_target_pairs={{0,2},{2,4},{4,6},{6,8},{8,10},{10,12},{12,14},{14,0},{1,3},{3,5},... | collective-permute-start | bytes 663560 | tf_op jit(solution)/shard_map/ppermute | solution.py:218
  22.5 0.0 collective-permute-done.3
  22.5 4.6 %collective-permute-start.5 = (bf16[2,16,3456]{2,1,0:T(8,128)(2,1)S(1)}, bf16[2,16,3456]{2,1,0:T(8,128)(2,1)S(1)}, u32[]{:S(2)}, u32[]{:S(2)}) collective-permute-start(bf16[2,16,3456]{2,1,0:T(8,128)(2,1)S(1)} %collective-permute-done.3), channel_id=1, source_target_pairs={{0,14},{2,0},{4,2},{6,4},{8,6},{10,8},{12,10},{14,12},{1,15},{3,1}... | collective-permute-start | bytes 663560 | tf_op jit(solution)/shard_map/ppermute | solution.py:223
  27.1 2.4 %collective-permute-done.4 = bf16[2,16,3456]{2,1,0:T(8,128)(2,1)S(1)} collective-permute-done((bf16[2,16,3456]{2,1,0:T(8,128)(2,1)S(1)}, bf16[2,16,3456]{2,1,0:T(8,128)(2,1)S(1)}, u32[]{:S(2)}, u32[]{:S(2)}) %collective-permute-start.4) | collective-permute-done | bytes 221216 | tf_op jit(solution)/shard_map/ppermute | solution.py:218
  29.5 1.9 %collective-permute-start.6 = (bf16[2,16,3456]{2,1,0:T(8,128)(2,1)S(1)}, bf16[2,16,3456]{2,1,0:T(8,128)(2,1)S(1)}, u32[]{:S(2)}, u32[]{:S(2)}) collective-permute-start(bf16[2,16,3456]{2,1,0:T(8,128)(2,1)S(1)} %collective-permute-done.4), channel_id=1, source_target_pairs={{0,2},{2,4},{4,6},{6,8},{8,10},{10,12},{12,14},{14,0},{1,3},{3,5},... | collective-permute-start | bytes 663560 | tf_op jit(solution)/shard_map/ppermute | solution.py:218
  31.5 12.4 %collective-permute-start.7 = (bf16[5,2,16,3456]{3,2,1,0:T(8,128)(2,1)S(1)}, bf16[5,2,16,3456]{3,2,1,0:T(8,128)(2,1)S(1)}, u32[]{:S(2)}, u32[]{:S(2)}) collective-permute-start(bf16[5,2,16,3456]{3,2,1,0:T(8,128)(2,1)S(1)} %bitcast_dynamic-update-slice_fusion.near.refs_0_), channel_id=1, source_target_pairs={{0,1},{1,0},{2,3},{3,2},{4,5},{5,4},{6,7},{7,6},{8,9},{9,8},{10,11... | collective-permute-start | bytes 3317768 | tf_op jit(solution)/shard_map/ppermute | solution.py:214
  43.9 0.0 collective-permute-done.5
  43.9 0.0 collective-permute-done.6
  43.9 0.1 pad_maximum_fusion.far.refs_1_
  44.0 7.0 %collective-permute-start.8 = (bf16[3,2,16,3456]{3,2,1,0:T(8,128)(2,1)S(1)}, bf16[3,2,16,3456]{3,2,1,0:T(8,128)(2,1)S(1)}, u32[]{:S(2)}, u32[]{:S(2)}) collective-permute-start(bf16[3,2,16,3456]{3,2,1,0:T(8,128)(2,1)S(1)} %pad_maximum_fusion.far.refs_1_), channel_id=1, source_target_pairs={{0,1},{1,0},{2,3},{3,2},{4,5},{5,4},{6,7},{7,6},{8,9},{9,8},{10,11... | collective-permute-start | bytes 1990664 | tf_op jit(solution)/shard_map/ppermute | solution.py:214
  51.0 0.0 copy-done
  51.0 2.0 %shard_map.88 = (f32[320,128]{1,0:T(8,128)S(1)}, f32[256,128]{1,0:T(8,128)S(1)}, bf16[3072,128]{1,0:T(8,128)(2,1)S(1)}) custom-call(s32[2]{0:T(128)S(1)} %pad_add_fusion.here_ref, bf16[5,2,16,3456]{3,2,1,0:T(8,128)(2,1)S(1)} %bitcast_dynamic-update-slice_fusion.near.refs_0_, bf16[3,2,16,3456]{3,2,1,0:T(8,128)(2,1)S(1)} %pad_maximum_fusion.far.refs_1_, ...), custom_call_target="tpu_custom_call" | custom-call | flops 402653184 | bytes 4194304 | tf_op jit(solution)/shard_map/pallas_call | solution.py:269
  53.0 0.0 collective-permute-done.8.other_far.refs_3_
  53.0 0.0 collective-permute-done.7.other_near.refs_2_
  53.0 2.0 %shard_map.89 = bf16[256,512]{1,0:T(8,128)(2,1)S(1)} custom-call(s32[2]{0:T(128)S(1)} %pad_add_fusion.here_ref, bf16[5,2,16,3456]{3,2,1,0:T(8,128)(2,1)S(1)} %bitcast_dynamic-update-slice_fusion.near.refs_0_, bf16[3,2,16,3456]{3,2,1,0:T(8,128)(2,1)S(1)} %pad_maximum_fusion.far.refs_1_, ...), custom_call_target="tpu_custom_call" | custom-call | tf_op jit(solution)/shard_map/pallas_call | solution.py:282
  55.1 16.5 %all_to_all.15.parts_ref = bf16[32,8,512]{2,1,0:T(8,128)(2,1)S(1)} all-to-all(bf16[32,8,512]{2,1,0:T(8,128)(2,1)S(1)} %bitcast.41), channel_id=1, replica_groups=mesh['row'=32,'y'=8,'core'=2] {'row'}, dimensions={0} | all-to-all | bytes 524288 | tf_op jit(solution)/shard_map/all_to_all | solution.py:28
  71.6 0.1 shard_map.90
  71.6 15.9 %all_to_all.16 = bf16[32,8,512]{2,1,0:T(8,128)(2,1)S(1)} all-to-all(bf16[32,8,512]{2,1,0:T(8,128)(2,1)S(1)} %shard_map.90), channel_id=1, replica_groups=mesh['row'=32,'y'=8,'core'=2] {'row'}, dimensions={0} | all-to-all | bytes 524288 | tf_op jit(solution)/shard_map/all_to_all | solution.py:28
  87.5 5.5 %collective-permute-start.9 = (bf16[256,512]{1,0:T(8,128)(2,1)S(1)}, bf16[256,512]{1,0:T(8,128)(2,1)S(1)}, u32[]{:S(2)}, u32[]{:S(2)}) collective-permute-start(bf16[256,512]{1,0:T(8,128)(2,1)S(1)} %bitcast.38), channel_id=1, source_target_pairs={{0,1},{1,0},{2,3},{3,2},{4,5},{5,4},{6,7},{7,6},{8,9},{9,8},{10,11... | collective-permute-start | bytes 786440 | tf_op jit(solution)/shard_map/ppermute | solution.py:302
  93.0 0.6 shard_map.91
  93.6 0.5 collective-permute-done.9.other_ref
  94.2 1.9 %shard_map.92 = bf16[16,256,128]{2,1,0:T(8,128)(2,1)} custom-call(bf16[256,512]{1,0:T(8,128)(2,1)S(1)} %bitcast.40, bf16[256,512]{1,0:T(8,128)(2,1)S(1)} %collective-permute-done.9.other_ref, bf16[256,128]{1,0:T(8,128)(2,1)S(1)} %get-tuple-element.15.weights_ref, f32[320,128]{1,0:T(8,128)S(1)} %get-tuple-element.16.partial_ref, ...), custom_call_target="tpu_custom_call" | custom-call | tf_op jit(solution)/shard_map/pallas_call | solution.py:315
  96.0 0.0 copy-start.6
  96.1 0.0 copy-start.4
  96.1 0.0 copy-start.5
  96.1 6.8 %all-to-all-start.2 = ((bf16[16,256,128]{2,1,0:T(8,128)(2,1)}), bf16[16,256,128]{2,1,0:T(8,128)(2,1)S(1)}, u32[]{:S(2)}, u32[]{:S(2)}) async-start(bf16[16,256,128]{2,1,0:T(8,128)(2,1)} %shard_map.92), calls=%async_computation.2 | async-start | bytes 2097152 | tf_op jit(solution)/shard_map/all_to_all | solution.py:28
  102.9 0.0 copy-done.6
  102.9 0.0 copy-done.4
  102.9 0.0 copy-done.5
  102.9 0.1 subtract_divide_fusion
  103.1 27.8 %all-to-all-done.2 = bf16[16,256,128]{2,1,0:T(8,128)(2,1)S(1)} async-done(((bf16[16,256,128]{2,1,0:T(8,128)(2,1)}), bf16[16,256,128]{2,1,0:T(8,128)(2,1)S(1)}, u32[]{:S(2)}, u32[]{:S(2)}) %all-to-all-start.2) | async-done | bytes 1048608 | tf_op jit(solution)/shard_map/all_to_all | solution.py:28
  130.9 1.3 fusion.4
  132.1 0.8 slice_bitcast_fusion.2
  (9 shorter events, 0.2 us)
Async XLA Ops:
  0.6 0.9 copy-start.2
  1.6 0.8 copy-start.3
  2.5 10.2 %collective-permute-start = (bf16[2,16,3456]{2,1,0:T(8,128)(2,1)S(1)}, bf16[2,16,3456]{2,1,0:T(8,128)(2,1)S(1)}, u32[]{:S(2)}, u32[]{:S(2)}) collective-permute-start(bf16[2,16,3456]{2,1,0:T(8,128)(2,1)S(1)} %shard_map.86), channel_id=1, source_target_pairs={{0,2},{2,4},{4,6},{6,8},{8,10},{10,12},{12,14},{14,0},{1,3},{3,5},... | collective-permute-start | bytes 663560 | tf_op jit(solution)/shard_map/ppermute | solution.py:218
  6.6 8.1 %collective-permute-start.1 = (bf16[2,16,3456]{2,1,0:T(8,128)(2,1)S(1)}, bf16[2,16,3456]{2,1,0:T(8,128)(2,1)S(1)}, u32[]{:S(2)}, u32[]{:S(2)}) collective-permute-start(bf16[2,16,3456]{2,1,0:T(8,128)(2,1)S(1)} %shard_map.86), channel_id=1, source_target_pairs={{0,14},{2,0},{4,2},{6,4},{8,6},{10,8},{12,10},{14,12},{1,15},{3,1}... | collective-permute-start | bytes 663560 | tf_op jit(solution)/shard_map/ppermute | solution.py:223
  10.5 1.0 copy-start.1
  12.7 7.9 %collective-permute-start.2 = (bf16[2,16,3456]{2,1,0:T(8,128)(2,1)S(1)}, bf16[2,16,3456]{2,1,0:T(8,128)(2,1)S(1)}, u32[]{:S(2)}, u32[]{:S(2)}) collective-permute-start(bf16[2,16,3456]{2,1,0:T(8,128)(2,1)S(1)} %collective-permute-done), channel_id=1, source_target_pairs={{0,2},{2,4},{4,6},{6,8},{8,10},{10,12},{12,14},{14,0},{1,3},{3,5},... | collective-permute-start | bytes 663560 | tf_op jit(solution)/shard_map/ppermute | solution.py:218
  14.7 7.9 %collective-permute-start.3 = (bf16[2,16,3456]{2,1,0:T(8,128)(2,1)S(1)}, bf16[2,16,3456]{2,1,0:T(8,128)(2,1)S(1)}, u32[]{:S(2)}, u32[]{:S(2)}) collective-permute-start(bf16[2,16,3456]{2,1,0:T(8,128)(2,1)S(1)} %collective-permute-done.1), channel_id=1, source_target_pairs={{0,14},{2,0},{4,2},{6,4},{8,6},{10,8},{12,10},{14,12},{1,15},{3,1}... | collective-permute-start | bytes 663560 | tf_op jit(solution)/shard_map/ppermute | solution.py:223
  19.3 31.7 %copy-start = (bf16[3072,128]{1,0:T(8,128)(2,1)S(1)}, bf16[3072,128]{1,0:T(8,128)(2,1)}, u32[]{:S(2)}) copy-start(bf16[3072,128]{1,0:T(8,128)(2,1)} %eig_hbm.1) | copy-start | bytes 2359300
  20.6 8.9 %collective-permute-start.4 = (bf16[2,16,3456]{2,1,0:T(8,128)(2,1)S(1)}, bf16[2,16,3456]{2,1,0:T(8,128)(2,1)S(1)}, u32[]{:S(2)}, u32[]{:S(2)}) collective-permute-start(bf16[2,16,3456]{2,1,0:T(8,128)(2,1)S(1)} %collective-permute-done.2), channel_id=1, source_target_pairs={{0,2},{2,4},{4,6},{6,8},{8,10},{10,12},{12,14},{14,0},{1,3},{3,5},... | collective-permute-start | bytes 663560 | tf_op jit(solution)/shard_map/ppermute | solution.py:218
  22.5 21.3 %collective-permute-start.5 = (bf16[2,16,3456]{2,1,0:T(8,128)(2,1)S(1)}, bf16[2,16,3456]{2,1,0:T(8,128)(2,1)S(1)}, u32[]{:S(2)}, u32[]{:S(2)}) collective-permute-start(bf16[2,16,3456]{2,1,0:T(8,128)(2,1)S(1)} %collective-permute-done.3), channel_id=1, source_target_pairs={{0,14},{2,0},{4,2},{6,4},{8,6},{10,8},{12,10},{14,12},{1,15},{3,1}... | collective-permute-start | bytes 663560 | tf_op jit(solution)/shard_map/ppermute | solution.py:223
  29.5 14.3 %collective-permute-start.6 = (bf16[2,16,3456]{2,1,0:T(8,128)(2,1)S(1)}, bf16[2,16,3456]{2,1,0:T(8,128)(2,1)S(1)}, u32[]{:S(2)}, u32[]{:S(2)}) collective-permute-start(bf16[2,16,3456]{2,1,0:T(8,128)(2,1)S(1)} %collective-permute-done.4), channel_id=1, source_target_pairs={{0,2},{2,4},{4,6},{6,8},{8,10},{10,12},{12,14},{14,0},{1,3},{3,5},... | collective-permute-start | bytes 663560 | tf_op jit(solution)/shard_map/ppermute | solution.py:218
  31.5 21.6 %collective-permute-start.7 = (bf16[5,2,16,3456]{3,2,1,0:T(8,128)(2,1)S(1)}, bf16[5,2,16,3456]{3,2,1,0:T(8,128)(2,1)S(1)}, u32[]{:S(2)}, u32[]{:S(2)}) collective-permute-start(bf16[5,2,16,3456]{3,2,1,0:T(8,128)(2,1)S(1)} %bitcast_dynamic-update-slice_fusion.near.refs_0_), channel_id=1, source_target_pairs={{0,1},{1,0},{2,3},{3,2},{4,5},{5,4},{6,7},{7,6},{8,9},{9,8},{10,11... | collective-permute-start | bytes 3317768 | tf_op jit(solution)/shard_map/ppermute | solution.py:214
  44.0 9.0 %collective-permute-start.8 = (bf16[3,2,16,3456]{3,2,1,0:T(8,128)(2,1)S(1)}, bf16[3,2,16,3456]{3,2,1,0:T(8,128)(2,1)S(1)}, u32[]{:S(2)}, u32[]{:S(2)}) collective-permute-start(bf16[3,2,16,3456]{3,2,1,0:T(8,128)(2,1)S(1)} %pad_maximum_fusion.far.refs_1_), channel_id=1, source_target_pairs={{0,1},{1,0},{2,3},{3,2},{4,5},{5,4},{6,7},{7,6},{8,9},{9,8},{10,11... | collective-permute-start | bytes 1990664 | tf_op jit(solution)/shard_map/ppermute | solution.py:214
  87.5 6.7 %collective-permute-start.9 = (bf16[256,512]{1,0:T(8,128)(2,1)S(1)}, bf16[256,512]{1,0:T(8,128)(2,1)S(1)}, u32[]{:S(2)}, u32[]{:S(2)}) collective-permute-start(bf16[256,512]{1,0:T(8,128)(2,1)S(1)} %bitcast.38), channel_id=1, source_target_pairs={{0,1},{1,0},{2,3},{3,2},{4,5},{5,4},{6,7},{7,6},{8,9},{9,8},{10,11... | collective-permute-start | bytes 786440 | tf_op jit(solution)/shard_map/ppermute | solution.py:302
  96.0 6.8 %copy-start.6 = (f32[8]{0:T(128)S(1)}, f32[8]{0:T(128)}, u32[]{:S(2)}) copy-start(f32[8]{0:T(128)} %param.12) | copy-start | bytes 100
  96.1 6.8 %copy-start.4 = (f32[2048]{0:T(1024)S(1)}, f32[2048]{0:T(1024)}, u32[]{:S(2)}) copy-start(f32[2048]{0:T(1024)} %param.10) | copy-start | bytes 24580
  96.1 6.8 %copy-start.5 = (f32[2048]{0:T(1024)S(1)}, f32[2048]{0:T(1024)}, u32[]{:S(2)}) copy-start(f32[2048]{0:T(1024)} %param.11) | copy-start | bytes 24580
  96.1 34.7 %all-to-all-start.2 = ((bf16[16,256,128]{2,1,0:T(8,128)(2,1)}), bf16[16,256,128]{2,1,0:T(8,128)(2,1)S(1)}, u32[]{:S(2)}, u32[]{:S(2)}) async-start(bf16[16,256,128]{2,1,0:T(8,128)(2,1)} %shard_map.92), calls=%async_computation.2 | async-start | bytes 2097152 | tf_op jit(solution)/shard_map/all_to_all | solution.py:28
